TPU v7x, 256 devices: a whole 4x4x8 slice. The times are simulated.
256 devices in a mesh: visit: 8 (over z), prow: 4 (over y), pcol: 8 (over x, core).
Axes of the slice: x: 4, y: 4, z: 8, core: 2. Of those that a mesh axis runs over, the one named last changes fastest.
Arguments:
- stamps: float32 [2048, 36864], P(('visit', 'prow', 'pcol')), may hold values from -8 to 8
- variance: float32 [2048, 128, 128], P(('visit', 'prow', 'pcol')), may hold values from 0.5 to 8
- coefficients: float32 [2048, 9], P(('visit', 'prow', 'pcol')), may hold values from -2 to 2
- band_offsets: int32 [2048, 2], P(('visit', 'prow', 'pcol')), may hold values from 2 to 31
- shifts: float32 [2048, 2], P(('visit', 'prow', 'pcol')), may hold values from 0 to 1
- destination: int32 [2048], P(('visit', 'prow', 'pcol')), may hold values from 0 to 31, as said below
- position: int32 [2048], P(('visit', 'prow', 'pcol')), may hold values from 0 to 15
- psf_taps: float32 [17], replicated, may hold values from 0.1 to 1
Outputs:
- coadd: float32 [2048, 4096], P('prow', 'pcol')
- detection: float32 [2048, 4096], P('prow', 'pcol')
Inputs may be any that keep to these rules, and one draw needn't show every extreme that they name: `destination`: each device's blocks name patches 0 .. 31; no device sends more than 2 of its blocks to one patch, and in every visit group one patch receives exactly 2 blocks from every device of that group.
All inputs are finite; a program needn't handle non-finite values.
Results may differ from a plain program's by a relative error of at most 0.0003.
Values sent between devices are 32-bit elements; how exact they have to be, the bound alone decides.
A program may use at most 64 MiB of HBM per device.

v0:
```python
import math

import jax
import jax.numpy as jnp
from jax import lax
from jax.experimental import pallas as pl
from jax.experimental.pallas import tpu as pltpu
from jax.sharding import PartitionSpec as P

MESH = pl.DeviceIdType.MESH
NB = 8
S = 192
B = 128
KR = 15
RF = 8
NZ = 8
NY = 4
NP = 8
NPLANE = NY * NP
TILES = 512
LANES = 128
WIDTHS = (1.0, 2.0, 4.0)
TAPS = (-2, -1, 0, 1, 2, 3)
CHUNK = 264
FIRST = 128
BF = jnp.bfloat16
F32 = jnp.float32


def norms(width):
    lags = range(-KR, KR + 1)
    bell = math.sqrt(sum(math.exp(-((t / width) ** 2)) for t in lags))
    quad = math.sqrt(sum((t / width) ** 4 * math.exp(-((t / width) ** 2)) for t in lags))
    return bell, quad


def split(x):
    hi = x.astype(BF)
    return hi, (x - hi.astype(F32)).astype(BF)


def mm(a, b):
    return jnp.dot(a, b, preferred_element_type=F32)


def sinc(x):
    scaled = math.pi * x
    return jnp.where(x == 0.0, 1.0, jnp.sin(scaled) / jnp.where(x == 0.0, 1.0, scaled))


def lanczos_weights(shift):
    lane = lax.broadcasted_iota(jnp.int32, (NB, LANES), 1).astype(F32)
    x = lane + float(TAPS[0]) - shift
    return jnp.where(jnp.abs(x) < 3.0, sinc(x) * sinc(x / 3.0), 0.0)


def factor_rows(place, weights):
    bells = [jnp.zeros((NB, LANES), F32) for _ in WIDTHS]
    quads = [jnp.zeros((NB, LANES), F32) for _ in WIDTHS]
    for index, tap in enumerate(TAPS):
        lag = place - float(tap + KR)
        weight = jnp.where(jnp.abs(lag) <= float(KR), weights[:, index : index + 1], 0.0)
        for w, width in enumerate(WIDTHS):
            bell_norm, quad_norm = norms(width)
            ratio = lag * (1.0 / width)
            term = weight * jnp.exp(-0.5 * ratio * ratio)
            bells[w] = bells[w] + term * (1.0 / bell_norm)
            quads[w] = quads[w] + ratio * ratio * term * (1.0 / quad_norm)
    return bells, quads


def make_bases(coef_ref, off_ref, shift_ref, base_ref):
    offsets = off_ref[...].astype(F32)
    shifts = shift_ref[...]
    coef = coef_ref[...]
    lane_int = lax.broadcasted_iota(jnp.int32, (NB, LANES), 1)
    lane = lane_int.astype(F32)
    col_weights = lanczos_weights(shifts[:, 1:2])
    row_weights = lanczos_weights(shifts[:, 0:1])
    place = jnp.where(lane_int == 0, 0.0, float(LANES) - lane)
    bells, quads = factor_rows(place - offsets[:, 1:2], col_weights)
    for w in range(3):
        base_ref[2 * w] = bells[w]
        base_ref[2 * w + 1] = quads[w]
    for d, delta in enumerate((0.0, -1.0, 1.0)):
        bells, quads = factor_rows(2.0 * lane + delta - offsets[:, 0:1], row_weights)
        for w in range(3):
            first = coef[:, 3 * w : 3 * w + 1]
            second = coef[:, 3 * w + 1 : 3 * w + 2]
            third = coef[:, 3 * w + 2 : 3 * w + 3]
            base_ref[6 + 6 * d + 2 * w] = first * bells[w] + second * quads[w]
            base_ref[6 + 6 * d + 2 * w + 1] = third * bells[w]


def skew(row, count):
    return pltpu.roll(jnp.broadcast_to(row, (count, LANES)), 0, 1, stride=1, stride_axis=0)


def warp_block(k, stamps_ref, base_ref, mh, ml, lh, ll, zb, flux_ref):
    r_iota = lax.broadcasted_iota(jnp.int32, (LANES, LANES), 0)
    c_iota = lax.broadcasted_iota(jnp.int32, (LANES, LANES), 1)
    lower = r_iota >= c_iota
    for j in range(6):
        cols = slice(j * LANES, (j + 1) * LANES)
        full = skew(base_ref[j, pl.ds(k, 1), :], LANES)
        hi, lo = split(jnp.where(lower, full, 0.0))
        mh[64:192, cols] = hi
        ml[64:192, cols] = lo
        hi, lo = split(jnp.where(lower[0:64], 0.0, full[0:64]))
        mh[192:256, cols] = hi
        ml[192:256, cols] = lo
        for d, spots in enumerate((((0, 0), (1, 1)), ((1, 0),), ((0, 1),))):
            hi, lo = split(skew(base_ref[6 + 6 * d + j, pl.ds(k, 1), :], 64))
            for e, f in spots:
                at = (f * 6 + j) * LANES
                lh[e * 64 : (e + 1) * 64, at : at + LANES] = hi
                ll[e * 64 : (e + 1) * 64, at : at + LANES] = lo
    rows_a = stamps_ref[pl.ds(k, 96, 24), :]
    rows_b = stamps_ref[pl.ds(8 + k, 96, 24), :]
    rows_c = stamps_ref[pl.ds(16 + k, 96, 24), :]
    for f, (left, right, start) in enumerate(((rows_a, rows_b, 64), (rows_b, rows_c, 0))):
        xh, xl = split(jnp.concatenate([left, right], axis=1))
        z = mm(xh, mh[start : start + 256, :]) + mm(xl, mh[start : start + 256, :])
        z = z + mm(xh, ml[start : start + 256, :])
        zh, zl = split(z)
        for j in range(6):
            at = (f * 6 + j) * LANES
            zb[at : at + 96, 0:LANES] = zh[:, j * LANES : (j + 1) * LANES]
            zb[at : at + 96, LANES : 2 * LANES] = zl[:, j * LANES : (j + 1) * LANES]
    both = mm(lh[...], zb[...])
    out = both[:, 0:LANES] + both[:, LANES:] + mm(ll[...], zb[:, 0:LANES])
    flux_ref[k, 0] = out[0:64]
    flux_ref[k, 1] = out[64:128]


def filter_blocks(taps_ref, transposed):
    r_iota = lax.broadcasted_iota(jnp.int32, (LANES, LANES), 0)
    c_iota = lax.broadcasted_iota(jnp.int32, (LANES, LANES), 1)
    lag = c_iota - r_iota if transposed else r_iota - c_iota
    result = []
    for shift in (-LANES, 0, LANES):
        band = jnp.zeros((LANES, LANES), F32)
        for tap in range(2 * RF + 1):
            band = jnp.where(lag + shift == tap - RF, taps_ref[tap], band)
        result.append(band)
    return result


def kernel(
    stamps_hbm, var_ref, coef_ref, off_ref, shift_ref, dest_ref, pos_ref, taps_ref,
    coadd_ref, det_ref,
    stamps_ref, base_ref, mh, ml, lh, ll, zb, flux_ref,
    ids_z, zw, zf, ids_row, ids_in, send_w, send_f, landed, onehot, data,
    sums, mate, half_ref, msg, ret, chunks, xbuf, ybuf, halo_out, halo_in,
    local_sem, zw_send, zw_recv, zi_send, zi_recv, zf_send, zf_recv,
    id_send, id_recv, in_send, in_recv, mate_send, mate_recv, ret_send, ret_recv,
    ring_send, ring_recv, halo_send, halo_recv,
):
    z = lax.axis_index("visit")
    y = lax.axis_index("prow")
    p = lax.axis_index("pcol")
    j = y * NP + p
    r = j // 2
    core = lax.rem(p, 2)
    fetch = pltpu.make_async_copy(stamps_hbm, stamps_ref, local_sem.at[0])
    fetch.start()

    barrier = pltpu.get_barrier_semaphore()

    @pl.loop(1, NZ)
    def _(d):
        pl.semaphore_signal(barrier, inc=1, device_id=(lax.rem(z + d, NZ), y, p), device_id_type=MESH)

    @pl.loop(1, NPLANE)
    def _(d):
        other = lax.rem(j + d, NPLANE)
        pl.semaphore_signal(barrier, inc=1, device_id=(z, other // NP, lax.rem(other, NP)), device_id_type=MESH)

    row_iota = lax.broadcasted_iota(jnp.int32, (NB, LANES), 0)
    ids = jnp.zeros((NB, LANES), F32)
    for b in range(NB):
        ids = jnp.where(row_iota == b, (dest_ref[b] * 16 + pos_ref[b]).astype(F32), ids)
    ids_z[z] = ids
    pl.semaphore_wait(barrier, NZ - 1 + NPLANE - 1)

    def z_ids(d):
        return pltpu.make_async_remote_copy(
            src_ref=ids_z.at[z], dst_ref=ids_z.at[z], send_sem=zi_send.at[d], recv_sem=zi_recv.at[z],
            device_id=(lax.rem(z + d, NZ), y, p), device_id_type=MESH)

    def z_var(d):
        to = lax.rem(z + d, NZ)
        return pltpu.make_async_remote_copy(
            src_ref=var_ref.at[:, pl.ds(pl.multiple_of(to * 16, 16), 16), :], dst_ref=zw.at[z],
            send_sem=zw_send.at[d], recv_sem=zw_recv.at[z], device_id=(to, y, p), device_id_type=MESH)

    def z_flux(e, d):
        to = lax.rem(z + d, NZ)
        return pltpu.make_async_remote_copy(
            src_ref=flux_ref.at[:, e, pl.ds(pl.multiple_of(to * 8, 8), 8), :], dst_ref=zf.at[e, z],
            send_sem=zf_send.at[e, d], recv_sem=zf_recv.at[e, z], device_id=(to, y, p), device_id_type=MESH)

    def wait_z(recv, dst):
        for d in range(1, NZ):
            source = lax.rem(z + d, NZ)
            pltpu.make_async_copy(dst.at[source], dst.at[source], recv.at[source]).wait()

    @pl.loop(1, NZ)
    def _(d):
        z_ids(d).start()

    @pl.loop(1, NZ)
    def _(d):
        z_var(d).start()

    own_var = pltpu.make_async_copy(
        var_ref.at[:, pl.ds(pl.multiple_of(z * 16, 16), 16), :], zw.at[z], local_sem.at[1])
    own_var.start()

    make_bases(coef_ref, off_ref, shift_ref, base_ref)
    mh[0:64, :] = jnp.zeros((64, 6 * LANES), BF)
    ml[0:64, :] = jnp.zeros((64, 6 * LANES), BF)
    mh[256:320, :] = jnp.zeros((64, 6 * LANES), BF)
    ml[256:320, :] = jnp.zeros((64, 6 * LANES), BF)
    zb[...] = jnp.zeros(zb.shape, BF)
    fetch.wait()

    @pl.loop(0, NB)
    def _(k):
        warp_block(k, stamps_ref, base_ref, mh, ml, lh, ll, zb, flux_ref)

    for e in range(2):

        @pl.loop(1, NZ)
        def _(d):
            z_flux(e, d).start()

    wait_z(zi_recv, ids_z)
    lane64 = lax.rem(lax.broadcasted_iota(jnp.int32, (64, LANES), 1), 64)
    row64 = lax.broadcasted_iota(jnp.int32, (64, LANES), 0)
    picked = jnp.where(lane64 == row64, ids_z[...].reshape(64, LANES), 0.0)
    ids_in[j] = jnp.broadcast_to(jnp.sum(picked, axis=0, keepdims=True), (8, LANES))

    def in_ids(d):
        other = lax.rem(j + d, NPLANE)
        return pltpu.make_async_remote_copy(
            src_ref=ids_in.at[j], dst_ref=ids_in.at[j], send_sem=id_send.at[d], recv_sem=id_recv.at[j],
            device_id=(z, other // NP, lax.rem(other, NP)), device_id_type=MESH)

    @pl.loop(1, NPLANE)
    def _(d):
        in_ids(d).start()

    def in_copy(buf, kind, row):
        other = 2 * row + kind
        return pltpu.make_async_remote_copy(
            src_ref=buf.at[row], dst_ref=landed.at[j], send_sem=in_send.at[other], recv_sem=in_recv.at[j],
            device_id=(z, other // NP, lax.rem(other, NP)), device_id_type=MESH)

    def own_copy(buf):
        return pltpu.make_async_copy(buf.at[r], landed.at[j], in_recv.at[j])

    def send_rows(buf, kind, first, step):
        @pl.loop(0, 16 // step)
        def _(d):
            row = lax.rem(r // step + d, 16 // step) * step + first
            here = 2 * row + kind == j

            @pl.when(here)
            def _():
                own_copy(buf).start()

            @pl.when(jnp.logical_not(here))
            def _():
                in_copy(buf, kind, row).start()

    wait_z(zw_recv, zw)
    own_var.wait()
    for source in range(NZ):
        weight = 1.0 / jnp.swapaxes(zw[source], 0, 1)
        send_w[:, source * NB : (source + 1) * NB, :] = weight
    send_rows(send_w, 1, 0, 1)

    @pl.loop(1, NPLANE)
    def _(d):
        other = lax.rem(j + d, NPLANE)
        pltpu.make_async_copy(ids_in.at[other], ids_in.at[other], id_recv.at[other]).wait()

    @pl.loop(0, 16)
    def _(pair):
        lane = lax.broadcasted_iota(jnp.int32, (8, LANES), 1)
        mixed = jnp.where(lane < 64, ids_in[2 * pair], ids_in[2 * pair + 1])
        tile = lax.broadcasted_iota(jnp.int32, (TILES, LANES), 0).astype(F32)
        onehot[:, pl.ds(pl.multiple_of(pair * LANES, LANES), LANES)] = jnp.where(
            tile == mixed[0:1], 1.0, 0.0).astype(BF)

    col_blocks = jnp.concatenate(filter_blocks(taps_ref, False), axis=0)
    row_blocks = filter_blocks(taps_ref, True)
    col_hi, col_lo = split(col_blocks)
    row_band = jnp.concatenate(
        [row_blocks[0][:, LANES - RF :], row_blocks[1], row_blocks[2][:, 0:RF]], axis=1)
    row_hi, row_lo = split(row_band)

    for e in range(2):
        wait_z(zf_recv.at[e], zf.at[e])
        zf[e, z] = flux_ref[:, e, pl.ds(pl.multiple_of(z * 8, 8), 8), :]
        for source in range(NZ):
            cells = jnp.swapaxes(zf[e, source], 0, 1)
            for q in range(8):
                at = slice(source * NB, (source + 1) * NB)
                send_f[2 * q + e, at, :] = cells[q] * send_w[2 * q + e, at, :]
        send_rows(send_f, 0, e, 2)

    @pl.loop(0, NPLANE)
    def _(d):
        other = lax.rem(j + d, NPLANE)
        pltpu.make_async_copy(landed.at[other], landed.at[other], in_recv.at[other]).wait()

    hi, lo = split(landed[...].reshape(NPLANE * 64, LANES))
    data[:, 0:LANES] = hi
    data[:, LANES:] = lo
    total = mm(onehot[...], data[...])
    sums[...] = total[:, 0:LANES] + total[:, LANES:]

    trade = pltpu.make_async_remote_copy(
        src_ref=sums.at[pl.ds(pl.multiple_of((1 - core) * 256, 256), 256), :], dst_ref=mate,
        send_sem=mate_send, recv_sem=mate_recv, device_id=(z, y, p + 1 - 2 * core), device_id_type=MESH)
    trade.start()
    half_ref[0:16, :] = jnp.zeros((16, LANES), F32)
    half_ref[272:288, :] = jnp.zeros((16, LANES), F32)
    own = sums[pl.ds(pl.multiple_of(core * 256, 256), 256), :]
    trade.wait_recv()
    theirs = mate[...]
    half_ref[16:272, :] = jnp.where(core == 0, own, theirs) / (1.0 + jnp.where(core == 0, theirs, own))

    patch = lax.rem(lax.broadcasted_iota(jnp.int32, (64, LANES), 0) // 4, NP)
    lane = lax.broadcasted_iota(jnp.int32, (64, LANES), 1)
    right = half_ref[pl.ds(32, 64, 4), :]
    left = half_ref[pl.ds(3, 64, 4), :]
    beside = jnp.where((lane < RF) & (patch < NP - 1), right, 0.0)
    beside = jnp.where((lane >= LANES - RF) & (patch > 0), left, beside)
    for m in range(16):
        msg[m, 0:16, :] = half_ref[16 + 16 * m : 32 + 16 * m, :]
        msg[m, 16:20, :] = beside[4 * m : 4 * m + 4]
        msg[m, 20:24, :] = jnp.zeros((4, LANES), F32)

    def ret_copy(m):
        return pltpu.make_async_remote_copy(
            src_ref=msg.at[m], dst_ref=ret.at[r], send_sem=ret_send.at[m], recv_sem=ret_recv.at[r],
            device_id=(z, 2 * core + m // 8, lax.rem(m, 8)), device_id_type=MESH)

    def each_owner(far, near):
        @pl.loop(0, 16)
        def _(d):
            m = lax.rem(r + d, 16)
            here = jnp.logical_and(2 * core + m // 8 == y, lax.rem(m, 8) == p)

            @pl.when(here)
            def _():
                near(m)

            @pl.when(jnp.logical_not(here))
            def _():
                far(m)

    each_owner(
        lambda m: ret_copy(m).start(),
        lambda m: pltpu.make_async_copy(msg.at[m], ret.at[r], ret_recv.at[r]).start())

    @pl.loop(0, 16)
    def _(s):
        pltpu.make_async_copy(ret.at[s], ret.at[s], ret_recv.at[s]).wait()

    got = jnp.swapaxes(ret[...], 0, 1)
    mine = chunks.at[z]
    for t in range(16):
        mine[16 * t : 16 * t + 16, :] = got[t]
    packed = jnp.zeros((8, LANES), F32)
    for g in range(8):
        packed = packed + pltpu.roll(got[16 + g // 2, 8 * (g % 2) : 8 * (g % 2) + 8, :], (8 + 16 * g) % LANES, 1)
    mine[256:264, :] = packed

    parts = ((0, FIRST), (FIRST, CHUNK - FIRST))

    def ring(way, step, part):
        which = lax.rem(z - step + NZ, NZ) if way == 0 else lax.rem(z + step, NZ)
        to = lax.rem(z + 1, NZ) if way == 0 else lax.rem(z + NZ - 1, NZ)
        at, size = parts[part]
        ref = chunks.at[which, pl.ds(at, size), :]
        return pltpu.make_async_remote_copy(
            src_ref=ref, dst_ref=ref, send_sem=ring_send.at[way, step, part],
            recv_sem=ring_recv.at[way, step, part], device_id=(to, y, p), device_id_type=MESH)

    def came(way, step, part):
        which = lax.rem(z - step - 1 + NZ, NZ) if way == 0 else lax.rem(z + step + 1, NZ)
        at, size = parts[part]
        ref = chunks.at[which, pl.ds(at, size), :]
        pltpu.make_async_copy(ref, ref, ring_recv.at[way, step, part]).wait()

    def filter_chunk(which):
        chunk = chunks[which]
        lane8 = lax.broadcasted_iota(jnp.int32, (8, LANES), 1)
        for pr in range(4):
            beside = []
            for h in range(2):
                rolled = pltpu.roll(chunk[256:264], (LANES - 8 - 16 * (2 * pr + h)) % LANES, 1)
                beside.append(jnp.where((lane8 < RF) | (lane8 >= LANES - RF), rolled, 0.0))
            beside = jnp.concatenate(beside, axis=0)
            tiles = [chunk[(4 * pr + pc) * 16 : (4 * pr + pc) * 16 + 16] for pc in range(4)]
            at = pl.ds(pl.multiple_of(pr * 128 + which * 16, 16), 16)
            for pc in range(4):
                coadd_ref[at, pc * LANES : (pc + 1) * LANES] = tiles[pc]
            around = [beside, *tiles, beside]
            for pc in range(4):
                hi, lo = split(jnp.concatenate(around[pc : pc + 3], axis=1))
                xbuf[pc * 64 + pr * 16 : pc * 64 + pr * 16 + 16, :] = hi
                xbuf[256 + pc * 64 + pr * 16 : 256 + pc * 64 + pr * 16 + 16, :] = lo
        got = mm(xbuf[...], col_hi)
        got = got[0:256] + got[256:512] + mm(xbuf[0:256, :], col_lo)
        for pc in range(4):
            for pr in range(4):
                at = pl.ds(pl.multiple_of(RF + pr * 128 + which * 16, 8), 16)
                ybuf[at, pc * LANES : (pc + 1) * LANES] = got[pc * 64 + pr * 16 : pc * 64 + pr * 16 + 16]

    for part in range(2):
        ring(0, 0, part).start()
        ring(1, 0, part).start()
    filter_chunk(z)
    for step in range(1, 4):
        for part in range(2):
            for way in range(2):
                came(way, step - 1, part)
                if step < 3 or part == way:
                    ring(way, step, part).start()
                elif step == 3:
                    pass
        filter_chunk(lax.rem(z - step + NZ, NZ))
        filter_chunk(lax.rem(z + step, NZ))
    came(0, 3, 0)
    came(1, 3, 1)
    filter_chunk(lax.rem(z + 4, NZ))

    halo_out[0] = ybuf[RF : 2 * RF, :]
    halo_out[1] = ybuf[512 : 512 + RF, :]

    def halo(side):
        return pltpu.make_async_remote_copy(
            src_ref=halo_out.at[side], dst_ref=halo_in.at[1 - side], send_sem=halo_send.at[side],
            recv_sem=halo_recv.at[1 - side], device_id=(z, y - 1 + 2 * side, p), device_id_type=MESH)

    for side in range(2):
        there = y > 0 if side == 0 else y < NY - 1

        @pl.when(there)
        def _():
            halo(side).start()

    for side in range(2):
        there = y > 0 if side == 0 else y < NY - 1
        rows = slice(0, RF) if side == 0 else slice(512 + RF, 512 + 2 * RF)

        @pl.when(there)
        def _():
            halo(1 - side).wait_recv()
            ybuf[rows, :] = halo_in[side]

        @pl.when(jnp.logical_not(there))
        def _():
            ybuf[rows, :] = jnp.zeros((RF, 512), F32)

    for t in range(4):
        yh, yl = split(ybuf[t * 128 : t * 128 + 128 + 2 * RF, :])
        det_ref[t * 128 : (t + 1) * 128, :] = mm(row_hi, yh) + mm(row_hi, yl) + mm(row_lo, yh)

    for side in range(2):
        there = y > 0 if side == 0 else y < NY - 1

        @pl.when(there)
        def _():
            halo(side).wait_send()

    for way in range(2):
        for step in range(4):
            for part in range(2):
                if step < 3 or part == way:
                    ring(way, step, part).wait_send()
    each_owner(lambda m: ret_copy(m).wait_send(), lambda m: None)
    trade.wait_send()

    @pl.loop(0, 16)
    def _(row):
        for kind, buf in ((0, send_f), (1, send_w)):

            @pl.when(2 * row + kind != j)
            def _():
                in_copy(buf, kind, row).wait_send()

    @pl.loop(1, NPLANE)
    def _(d):
        in_ids(d).wait_send()

    @pl.loop(1, NZ)
    def _(d):
        z_ids(d).wait_send()
        z_var(d).wait_send()
        for e in range(2):
            z_flux(e, d).wait_send()


def body(stamps, variance, coefficients, band_offsets, shifts, destination, position, psf_taps):
    cells = stamps.reshape(NB, S * S // LANES, LANES).transpose(1, 0, 2).reshape(NB * S * S // LANES, LANES)
    vmem = pl.BlockSpec(memory_space=pltpu.VMEM)
    smem = pl.BlockSpec(memory_space=pltpu.SMEM)
    hbm = pl.BlockSpec(memory_space=pl.ANY)
    dma = pltpu.SemaphoreType.DMA
    scratch = [
        pltpu.VMEM((NB * S * S // LANES, LANES), F32),
        pltpu.VMEM((24, NB, LANES), F32),
        pltpu.VMEM((320, 768), BF),
        pltpu.VMEM((320, 768), BF),
        pltpu.VMEM((LANES, 12 * LANES), BF),
        pltpu.VMEM((LANES, 12 * LANES), BF),
        pltpu.VMEM((12 * LANES, 2 * LANES), BF),
        pltpu.VMEM((NB, 2, 64, LANES), F32),
        pltpu.VMEM((NZ, NB, LANES), F32),
        pltpu.VMEM((NZ, NB, 16, LANES), F32),
        pltpu.VMEM((2, NZ, NB, 8, LANES), F32),
        pltpu.VMEM((8, LANES), F32),
        pltpu.VMEM((NPLANE, 8, LANES), F32),
        pltpu.VMEM((16, 64, LANES), F32),
        pltpu.VMEM((16, 64, LANES), F32),
        pltpu.VMEM((NPLANE, 64, LANES), F32),
        pltpu.VMEM((TILES, NPLANE * 64), BF),
        pltpu.VMEM((NPLANE * 64, 2 * LANES), BF),
        pltpu.VMEM((TILES, LANES), F32),
        pltpu.VMEM((TILES // 2, LANES), F32),
        pltpu.VMEM((288, LANES), F32),
        pltpu.VMEM((16, 24, LANES), F32),
        pltpu.VMEM((16, 24, LANES), F32),
        pltpu.VMEM((NZ, CHUNK, LANES), F32),
        pltpu.VMEM((512, 3 * LANES), BF),
        pltpu.VMEM((512 + 2 * RF, 512), F32),
        pltpu.VMEM((2, RF, 512), F32),
        pltpu.VMEM((2, RF, 512), F32),
        dma((2,)),
        dma((NZ,)), dma((NZ,)), dma((NZ,)), dma((NZ,)), dma((2, NZ)), dma((2, NZ)),
        dma((NPLANE,)), dma((NPLANE,)), dma((NPLANE,)), dma((NPLANE,)), dma, dma, dma((16,)), dma((16,)),
        dma((2, 4, 2)), dma((2, 4, 2)), dma((2,)), dma((2,)),
    ]
    return pl.pallas_call(
        kernel,
        out_shape=(jax.ShapeDtypeStruct((512, 512), F32), jax.ShapeDtypeStruct((512, 512), F32)),
        in_specs=[hbm, hbm, vmem, vmem, vmem, smem, smem, smem],
        out_specs=(vmem, vmem),
        scratch_shapes=scratch,
        compiler_params=pltpu.CompilerParams(
            collective_id=0, has_side_effects=True, vmem_limit_bytes=40 * 1024 * 1024),
    )(cells, variance, coefficients, band_offsets, shifts, destination, position, psf_taps)


def solution(mesh):
    placed = (
        P(("visit", "prow", "pcol"), None),
        P(("visit", "prow", "pcol"), None, None),
        P(("visit", "prow", "pcol"), None),
        P(("visit", "prow", "pcol"), None),
        P(("visit", "prow", "pcol"), None),
        P(("visit", "prow", "pcol")),
        P(("visit", "prow", "pcol")),
        P(),
    )
    return jax.shard_map(
        body,
        mesh=mesh,
        in_specs=placed,
        out_specs=(P("prow", "pcol"), P("prow", "pcol")),
        check_vma=False,
    )
```

profile of v0, /device:TPU:2, one launch (start us, length us, event | category | flops | bytes accessed | tf_op | source)
XLA Modules:
  0.0 85.0 jit_solution(12528179797796433134)
XLA Ops:
  0.6 0.8 copy.10.off_ref
  1.4 0.8 copy.11.shift_ref
  2.1 0.0 copy-start
  2.1 1.3 %copy-done = f32[8,36864]{1,0:T(8,128)S(1)} copy-done((f32[8,36864]{1,0:T(8,128)S(1)}, f32[8,36864]{1,0:T(8,128)}, u32[]{:S(2)}) %copy-start) | copy-done | bytes 1179672
  3.4 0.0 copy-start.1
  3.4 1.0 %copy-done.1 = f32[8,128,128]{2,1,0:T(8,128)S(1)} copy-done((f32[8,128,128]{2,1,0:T(8,128)S(1)}, f32[8,128,128]{2,1,0:T(8,128)}, u32[]{:S(2)}) %copy-start.1) | copy-done | bytes 524312
  4.5 0.0 copy-start.2
  4.5 0.7 copy-done.2
  5.1 0.0 copy-start.3
  5.1 0.7 copy-done.3
  5.8 0.0 copy-start.4
  5.8 0.7 copy-done.4
  6.4 0.0 copy-start.5
  6.5 0.7 copy-done.5
  7.1 75.9 %shard_map.95 = (f32[512,512]{1,0:T(8,128)S(1)}, f32[512,512]{1,0:T(8,128)S(1)}) custom-call(f32[2304,128]{1,0:T(8,128)S(1)} %bitcast.5, f32[8,128,128]{2,1,0:T(8,128)S(1)} %copy-done.1, f32[8,9]{1,0:T(8,128)S(1)} %copy-done.2, s32[8,2]{1,0:T(8,128)S(1)} %copy.10.off_ref, f32[8,2]{1,0:T(8,128)S(1)} %copy.11.shift_ref, s32[8]{0:T(128)S(1)} %copy-done.3, ...), custom_call_target="tpu_custom_call" | custom-call | tf_op jit(solution)/shard_map/pallas_call | solution.py:550
  83.0 1.0 %copy.14 = f32[512,512]{1,0:T(8,128)} copy(f32[512,512]{1,0:T(8,128)S(1)} %get-tuple-element.4) | data formatting | bytes 2097152
  84.0 1.0 %copy.15 = f32[512,512]{1,0:T(8,128)} copy(f32[512,512]{1,0:T(8,128)S(1)} %get-tuple-element.5) | data formatting | bytes 2097152
Async XLA Ops:
  2.1 1.3 %copy-start = (f32[8,36864]{1,0:T(8,128)S(1)}, f32[8,36864]{1,0:T(8,128)}, u32[]{:S(2)}) copy-start(f32[8,36864]{1,0:T(8,128)} %param.8) | copy-start | bytes 3538948
  3.4 1.0 %copy-start.1 = (f32[8,128,128]{2,1,0:T(8,128)S(1)}, f32[8,128,128]{2,1,0:T(8,128)}, u32[]{:S(2)}) copy-start(f32[8,128,128]{2,1,0:T(8,128)} %var_ref.1) | copy-start | bytes 1572868
  4.5 0.7 copy-start.2
  5.1 0.7 copy-start.3
  5.8 0.7 copy-start.4
  6.4 0.7 copy-start.5
where the time goes:
time: 85.2 us; the launch traced here: 85 us
  Pallas kernels  75.9 us (89%)
  local copies, waits for them, and re-layouts  8.41 us (10%)
    pallas_call x1, Pallas kernels, body(): pl.pallas_call(kernel, out_shape=(jax.ShapeDtypeStruct((512, 512), F32),...  75.9 us
    unnamed x16, local copies, waits for them, and re-layouts  8.41 us

commit v1 on v0

--- a/solution.py
+++ b/solution.py
@@ -22,7 +22,7 @@
 WIDTHS = (1.0, 2.0, 4.0)
 TAPS = (-2, -1, 0, 1, 2, 3)
 CHUNK = 264
-FIRST = 128
+PARTS = ((0, 64), (64, 64), (128, 64), (192, 72))
 BF = jnp.bfloat16
 F32 = jnp.float32
 
@@ -70,24 +70,29 @@
 
 
 def make_bases(coef_ref, off_ref, shift_ref, base_ref):
-    offsets = off_ref[...].astype(F32)
-    shifts = shift_ref[...]
-    coef = coef_ref[...]
+    row = lax.broadcasted_iota(jnp.int32, (NB, LANES), 0)
+
+    def column(read):
+        result = jnp.zeros((NB, LANES), F32)
+        for b in range(NB):
+            result = jnp.where(row == b, read(b).astype(F32), result)
+        return result
+
     lane_int = lax.broadcasted_iota(jnp.int32, (NB, LANES), 1)
     lane = lane_int.astype(F32)
-    col_weights = lanczos_weights(shifts[:, 1:2])
-    row_weights = lanczos_weights(shifts[:, 0:1])
+    col_weights = lanczos_weights(column(lambda b: shift_ref[1, b]))
+    row_weights = lanczos_weights(column(lambda b: shift_ref[0, b]))
     place = jnp.where(lane_int == 0, 0.0, float(LANES) - lane)
-    bells, quads = factor_rows(place - offsets[:, 1:2], col_weights)
+    row_offset = column(lambda b: off_ref[0, b])
+    bells, quads = factor_rows(place - column(lambda b: off_ref[1, b]), col_weights)
     for w in range(3):
         base_ref[2 * w] = bells[w]
         base_ref[2 * w + 1] = quads[w]
+    coefs = [column(lambda b, i=i: coef_ref[b, i]) for i in range(9)]
     for d, delta in enumerate((0.0, -1.0, 1.0)):
-        bells, quads = factor_rows(2.0 * lane + delta - offsets[:, 0:1], row_weights)
+        bells, quads = factor_rows(2.0 * lane + delta - row_offset, row_weights)
         for w in range(3):
-            first = coef[:, 3 * w : 3 * w + 1]
-            second = coef[:, 3 * w + 1 : 3 * w + 2]
-            third = coef[:, 3 * w + 2 : 3 * w + 3]
+            first, second, third = coefs[3 * w : 3 * w + 3]
             base_ref[6 + 6 * d + 2 * w] = first * bells[w] + second * quads[w]
             base_ref[6 + 6 * d + 2 * w + 1] = third * bells[w]
 
@@ -147,14 +152,15 @@
 
 
 def kernel(
-    stamps_hbm, var_ref, coef_ref, off_ref, shift_ref, dest_ref, pos_ref, taps_ref,
-    coadd_ref, det_ref,
+    stamps_hbm, var_ref, coef_hbm, off_hbm, shift_hbm, dest_hbm, pos_hbm, taps_hbm,
+    coadd_hbm, rows_hbm,
+    coef_ref, off_ref, shift_ref, dest_ref, pos_ref, taps_ref,
     stamps_ref, base_ref, mh, ml, lh, ll, zb, flux_ref,
-    ids_z, zw, zf, ids_row, ids_in, send_w, send_f, landed, onehot, data,
-    sums, mate, half_ref, msg, ret, chunks, xbuf, ybuf, halo_out, halo_in,
-    local_sem, zw_send, zw_recv, zi_send, zi_recv, zf_send, zf_recv,
+    ids_z, zw, zf, ids_in, send_w, send_f, landed, onehot, data,
+    sums, mate, half_ref, msg, ret, chunks, xbuf, ybuf, coadd_ref,
+    seen, small_sem, local_sem, zw_send, zw_recv, zi_send, zi_recv, zf_send, zf_recv,
     id_send, id_recv, in_send, in_recv, mate_send, mate_recv, ret_send, ret_recv,
-    ring_send, ring_recv, halo_send, halo_recv,
+    ring_send, ring_recv, halo_send, halo_recv, out_sem,
 ):
     z = lax.axis_index("visit")
     y = lax.axis_index("prow")
@@ -162,26 +168,40 @@
     j = y * NP + p
     r = j // 2
     core = lax.rem(p, 2)
+    small = [
+        pltpu.make_async_copy(far, near, small_sem.at[i])
+        for i, (far, near) in enumerate((
+            (dest_hbm, dest_ref), (pos_hbm, pos_ref), (off_hbm, off_ref), (shift_hbm, shift_ref),
+            (coef_hbm, coef_ref), (taps_hbm, taps_ref)))
+    ]
+    for copy in small:
+        copy.start()
     fetch = pltpu.make_async_copy(stamps_hbm, stamps_ref, local_sem.at[0])
     fetch.start()
 
+    later = []
     barrier = pltpu.get_barrier_semaphore()
 
     @pl.loop(1, NZ)
     def _(d):
         pl.semaphore_signal(barrier, inc=1, device_id=(lax.rem(z + d, NZ), y, p), device_id_type=MESH)
 
-    @pl.loop(1, NPLANE)
-    def _(d):
-        other = lax.rem(j + d, NPLANE)
-        pl.semaphore_signal(barrier, inc=1, device_id=(z, other // NP, lax.rem(other, NP)), device_id_type=MESH)
-
+    @pl.loop(1, NY)
+    def _(d):
+        pl.semaphore_signal(barrier, inc=1, device_id=(z, lax.rem(y + d, NY), p), device_id_type=MESH)
+
+    @pl.loop(1, NP)
+    def _(d):
+        pl.semaphore_signal(barrier, inc=1, device_id=(z, y, lax.rem(p + d, NP)), device_id_type=MESH)
+
+    for copy in small:
+        copy.wait()
     row_iota = lax.broadcasted_iota(jnp.int32, (NB, LANES), 0)
     ids = jnp.zeros((NB, LANES), F32)
     for b in range(NB):
         ids = jnp.where(row_iota == b, (dest_ref[b] * 16 + pos_ref[b]).astype(F32), ids)
     ids_z[z] = ids
-    pl.semaphore_wait(barrier, NZ - 1 + NPLANE - 1)
+    pl.semaphore_wait(barrier, NZ + NY + NP - 3)
 
     def z_ids(d):
         return pltpu.make_async_remote_copy(
@@ -213,9 +233,20 @@
     def _(d):
         z_var(d).start()
 
+    @later.append
+    def _():
+        @pl.loop(1, NZ)
+        def _(d):
+            z_ids(d).wait_send()
+            z_var(d).wait_send()
+
     own_var = pltpu.make_async_copy(
         var_ref.at[:, pl.ds(pl.multiple_of(z * 16, 16), 16), :], zw.at[z], local_sem.at[1])
     own_var.start()
+
+    @pl.loop(1, NY)
+    def _(d):
+        pl.semaphore_signal(seen, inc=1, device_id=(z, lax.rem(y + d, NY), p), device_id_type=MESH)
 
     make_bases(coef_ref, off_ref, shift_ref, base_ref)
     mh[0:64, :] = jnp.zeros((64, 6 * LANES), BF)
@@ -235,6 +266,13 @@
         def _(d):
             z_flux(e, d).start()
 
+    @later.append
+    def _():
+        @pl.loop(1, NZ)
+        def _(d):
+            for e in range(2):
+                z_flux(e, d).wait_send()
+
     wait_z(zi_recv, ids_z)
     lane64 = lax.rem(lax.broadcasted_iota(jnp.int32, (64, LANES), 1), 64)
     row64 = lax.broadcasted_iota(jnp.int32, (64, LANES), 0)
@@ -247,9 +285,17 @@
             src_ref=ids_in.at[j], dst_ref=ids_in.at[j], send_sem=id_send.at[d], recv_sem=id_recv.at[j],
             device_id=(z, other // NP, lax.rem(other, NP)), device_id_type=MESH)
 
+    pl.semaphore_wait(seen, NY - 1)
+
     @pl.loop(1, NPLANE)
     def _(d):
         in_ids(d).start()
+
+    @later.append
+    def _():
+        @pl.loop(1, NPLANE)
+        def _(d):
+            in_ids(d).wait_send()
 
     def in_copy(buf, kind, row):
         other = 2 * row + kind
@@ -259,6 +305,16 @@
 
     def own_copy(buf):
         return pltpu.make_async_copy(buf.at[r], landed.at[j], in_recv.at[j])
+
+    @later.append
+    def _():
+        @pl.loop(0, 16)
+        def _(row):
+            for kind, buf in ((0, send_f), (1, send_w)):
+
+                @pl.when(2 * row + kind != j)
+                def _():
+                    in_copy(buf, kind, row).wait_send()
 
     def send_rows(buf, kind, first, step):
         @pl.loop(0, 16 // step)
@@ -295,11 +351,8 @@
             tile == mixed[0:1], 1.0, 0.0).astype(BF)
 
     col_blocks = jnp.concatenate(filter_blocks(taps_ref, False), axis=0)
-    row_blocks = filter_blocks(taps_ref, True)
     col_hi, col_lo = split(col_blocks)
-    row_band = jnp.concatenate(
-        [row_blocks[0][:, LANES - RF :], row_blocks[1], row_blocks[2][:, 0:RF]], axis=1)
-    row_hi, row_lo = split(row_band)
+    col_both = jnp.concatenate([col_hi, col_lo], axis=1)
 
     for e in range(2):
         wait_z(zf_recv.at[e], zf.at[e])
@@ -326,6 +379,7 @@
         src_ref=sums.at[pl.ds(pl.multiple_of((1 - core) * 256, 256), 256), :], dst_ref=mate,
         send_sem=mate_send, recv_sem=mate_recv, device_id=(z, y, p + 1 - 2 * core), device_id_type=MESH)
     trade.start()
+    later.append(trade.wait_send)
     half_ref[0:16, :] = jnp.zeros((16, LANES), F32)
     half_ref[272:288, :] = jnp.zeros((16, LANES), F32)
     own = sums[pl.ds(pl.multiple_of(core * 256, 256), 256), :]
@@ -367,6 +421,8 @@
         lambda m: ret_copy(m).start(),
         lambda m: pltpu.make_async_copy(msg.at[m], ret.at[r], ret_recv.at[r]).start())
 
+    later.append(lambda: each_owner(lambda m: ret_copy(m).wait_send(), lambda m: None))
+
     @pl.loop(0, 16)
     def _(s):
         pltpu.make_async_copy(ret.at[s], ret.at[s], ret_recv.at[s]).wait()
@@ -380,12 +436,11 @@
         packed = packed + pltpu.roll(got[16 + g // 2, 8 * (g % 2) : 8 * (g % 2) + 8, :], (8 + 16 * g) % LANES, 1)
     mine[256:264, :] = packed
 
-    parts = ((0, FIRST), (FIRST, CHUNK - FIRST))
 
     def ring(way, step, part):
         which = lax.rem(z - step + NZ, NZ) if way == 0 else lax.rem(z + step, NZ)
         to = lax.rem(z + 1, NZ) if way == 0 else lax.rem(z + NZ - 1, NZ)
-        at, size = parts[part]
+        at, size = PARTS[part]
         ref = chunks.at[which, pl.ds(at, size), :]
         return pltpu.make_async_remote_copy(
             src_ref=ref, dst_ref=ref, send_sem=ring_send.at[way, step, part],
@@ -393,9 +448,16 @@
 
     def came(way, step, part):
         which = lax.rem(z - step - 1 + NZ, NZ) if way == 0 else lax.rem(z + step + 1, NZ)
-        at, size = parts[part]
+        at, size = PARTS[part]
         ref = chunks.at[which, pl.ds(at, size), :]
         pltpu.make_async_copy(ref, ref, ring_recv.at[way, step, part]).wait()
+
+    def halo(side):
+        mine, theirs = (RF, 512 + RF) if side == 0 else (512, 0)
+        return pltpu.make_async_remote_copy(
+            src_ref=ybuf.at[pl.ds(mine, RF), :], dst_ref=ybuf.at[pl.ds(theirs, RF), :],
+            send_sem=halo_send.at[side], recv_sem=halo_recv.at[1 - side],
+            device_id=(z, y - 1 + 2 * side, p), device_id_type=MESH)
 
     def filter_chunk(which):
         chunk = chunks[which]
@@ -415,105 +477,127 @@
                 hi, lo = split(jnp.concatenate(around[pc : pc + 3], axis=1))
                 xbuf[pc * 64 + pr * 16 : pc * 64 + pr * 16 + 16, :] = hi
                 xbuf[256 + pc * 64 + pr * 16 : 256 + pc * 64 + pr * 16 + 16, :] = lo
-        got = mm(xbuf[...], col_hi)
-        got = got[0:256] + got[256:512] + mm(xbuf[0:256, :], col_lo)
+        got = mm(xbuf[0:256, :], col_both)
+        got = got[:, 0:LANES] + got[:, LANES:] + mm(xbuf[256:512, :], col_hi)
         for pc in range(4):
             for pr in range(4):
                 at = pl.ds(pl.multiple_of(RF + pr * 128 + which * 16, 8), 16)
                 ybuf[at, pc * LANES : (pc + 1) * LANES] = got[pc * 64 + pr * 16 : pc * 64 + pr * 16 + 16]
 
-    for part in range(2):
+        for pr in range(4):
+            at = pl.ds(pl.multiple_of(pr * 128 + which * 16, 16), 16)
+            pltpu.make_async_copy(coadd_ref.at[at, :], coadd_hbm.at[at, :], out_sem.at[0]).start()
+
+        @pl.when(jnp.logical_and(which == 0, y > 0))
+        def _():
+            halo(0).start()
+
+        @pl.when(jnp.logical_and(which == NZ - 1, y < NY - 1))
+        def _():
+            halo(1).start()
+
+    def passes(way, step, part):
+        return step < 3 or part // 2 == way
+
+    @later.append
+    def _():
+        for way in range(2):
+            for step in range(4):
+                for part in range(4):
+                    if passes(way, step, part):
+                        ring(way, step, part).wait_send()
+
+    def advance(step, part):
+        for way in range(2):
+            if passes(way, step - 1, part):
+                came(way, step - 1, part)
+                if step < 4 and passes(way, step, part):
+                    ring(way, step, part).start()
+
+    for part in range(4):
         ring(0, 0, part).start()
         ring(1, 0, part).start()
     filter_chunk(z)
-    for step in range(1, 4):
-        for part in range(2):
-            for way in range(2):
-                came(way, step - 1, part)
-                if step < 3 or part == way:
-                    ring(way, step, part).start()
-                elif step == 3:
-                    pass
-        filter_chunk(lax.rem(z - step + NZ, NZ))
-        filter_chunk(lax.rem(z + step, NZ))
-    came(0, 3, 0)
-    came(1, 3, 1)
+    for step in range(1, 5):
+        for part in range(4):
+            advance(step, part)
+            if step > 1 and part == 1:
+                filter_chunk(lax.rem(z - step + 1 + NZ, NZ))
+        if step > 1:
+            filter_chunk(lax.rem(z + step - 1, NZ))
     filter_chunk(lax.rem(z + 4, NZ))
-
-    halo_out[0] = ybuf[RF : 2 * RF, :]
-    halo_out[1] = ybuf[512 : 512 + RF, :]
-
-    def halo(side):
-        return pltpu.make_async_remote_copy(
-            src_ref=halo_out.at[side], dst_ref=halo_in.at[1 - side], send_sem=halo_send.at[side],
-            recv_sem=halo_recv.at[1 - side], device_id=(z, y - 1 + 2 * side, p), device_id_type=MESH)
 
     for side in range(2):
         there = y > 0 if side == 0 else y < NY - 1
-
-        @pl.when(there)
-        def _():
-            halo(side).start()
-
-    for side in range(2):
-        there = y > 0 if side == 0 else y < NY - 1
-        rows = slice(0, RF) if side == 0 else slice(512 + RF, 512 + 2 * RF)
+        at = 0 if side == 0 else 512 + RF
 
         @pl.when(there)
         def _():
             halo(1 - side).wait_recv()
-            ybuf[rows, :] = halo_in[side]
 
         @pl.when(jnp.logical_not(there))
         def _():
-            ybuf[rows, :] = jnp.zeros((RF, 512), F32)
-
+            ybuf[at : at + RF, :] = jnp.zeros((RF, 512), F32)
+
+    @later.append
+    def _():
+        for side in range(2):
+            there = y > 0 if side == 0 else y < NY - 1
+
+            @pl.when(there)
+            def _():
+                halo(side).wait_send()
+
+    rows_out = pltpu.make_async_copy(ybuf, rows_hbm, out_sem.at[1])
+    rows_out.start()
+    for left in later:
+        left()
+    pltpu.make_async_copy(coadd_ref, coadd_hbm, out_sem.at[0]).wait()
+    rows_out.wait()
+
+
+def filter_rows(taps_hbm, cells_hbm, rows_hbm, coadd_hbm, det_hbm, taps_ref, rows_ref, cells_ref, det_ref, in_sem, out_sem):
+    cells = pltpu.make_async_copy(cells_hbm, cells_ref, in_sem.at[5])
+    pieces = []
     for t in range(4):
-        yh, yl = split(ybuf[t * 128 : t * 128 + 128 + 2 * RF, :])
-        det_ref[t * 128 : (t + 1) * 128, :] = mm(row_hi, yh) + mm(row_hi, yl) + mm(row_lo, yh)
-
-    for side in range(2):
-        there = y > 0 if side == 0 else y < NY - 1
-
-        @pl.when(there)
-        def _():
-            halo(side).wait_send()
-
-    for way in range(2):
-        for step in range(4):
-            for part in range(2):
-                if step < 3 or part == way:
-                    ring(way, step, part).wait_send()
-    each_owner(lambda m: ret_copy(m).wait_send(), lambda m: None)
-    trade.wait_send()
-
-    @pl.loop(0, 16)
-    def _(row):
-        for kind, buf in ((0, send_f), (1, send_w)):
-
-            @pl.when(2 * row + kind != j)
-            def _():
-                in_copy(buf, kind, row).wait_send()
-
-    @pl.loop(1, NPLANE)
-    def _(d):
-        in_ids(d).wait_send()
-
-    @pl.loop(1, NZ)
-    def _(d):
-        z_ids(d).wait_send()
-        z_var(d).wait_send()
-        for e in range(2):
-            z_flux(e, d).wait_send()
+        at = pl.ds(t * 136, 136 if t < 3 else 120)
+        pieces.append(pltpu.make_async_copy(rows_hbm.at[at, :], rows_ref.at[at, :], in_sem.at[t]))
+    taps = pltpu.make_async_copy(taps_hbm, taps_ref, in_sem.at[4])
+    for copy in (taps, *pieces, cells):
+        copy.start()
+    taps.wait()
+    blocks = filter_blocks(taps_ref, True)
+    band = jnp.concatenate([blocks[0][:, LANES - RF :], blocks[1], blocks[2][:, 0:RF]], axis=1)
+    hi, lo = split(band)
+    pieces[0].wait()
+    results = []
+    for t in range(4):
+        if t < 3:
+            pieces[t + 1].wait()
+        yh, yl = split(rows_ref[t * 128 : t * 128 + 128 + 2 * RF, :])
+        det_ref[t * 128 : (t + 1) * 128, :] = mm(hi, yh) + mm(hi, yl) + mm(lo, yh)
+        at = pl.ds(t * 128, 128)
+        results.append(pltpu.make_async_copy(det_ref.at[at, :], det_hbm.at[at, :], out_sem.at[t]))
+        results[-1].start()
+        if t == 1:
+            cells.wait()
+            results.append(pltpu.make_async_copy(cells_ref, coadd_hbm, out_sem.at[4]))
+            results[-1].start()
+    for copy in results:
+        copy.wait()
 
 
 def body(stamps, variance, coefficients, band_offsets, shifts, destination, position, psf_taps):
     cells = stamps.reshape(NB, S * S // LANES, LANES).transpose(1, 0, 2).reshape(NB * S * S // LANES, LANES)
-    vmem = pl.BlockSpec(memory_space=pltpu.VMEM)
-    smem = pl.BlockSpec(memory_space=pltpu.SMEM)
     hbm = pl.BlockSpec(memory_space=pl.ANY)
     dma = pltpu.SemaphoreType.DMA
     scratch = [
+        pltpu.SMEM((NB, 9), F32),
+        pltpu.SMEM((2, NB), jnp.int32),
+        pltpu.SMEM((2, NB), F32),
+        pltpu.SMEM((NB,), jnp.int32),
+        pltpu.SMEM((NB,), jnp.int32),
+        pltpu.SMEM((2 * RF + 1,), F32),
         pltpu.VMEM((NB * S * S // LANES, LANES), F32),
         pltpu.VMEM((24, NB, LANES), F32),
         pltpu.VMEM((320, 768), BF),
@@ -525,7 +609,6 @@
         pltpu.VMEM((NZ, NB, LANES), F32),
         pltpu.VMEM((NZ, NB, 16, LANES), F32),
         pltpu.VMEM((2, NZ, NB, 8, LANES), F32),
-        pltpu.VMEM((8, LANES), F32),
         pltpu.VMEM((NPLANE, 8, LANES), F32),
         pltpu.VMEM((16, 64, LANES), F32),
         pltpu.VMEM((16, 64, LANES), F32),
@@ -540,22 +623,31 @@
         pltpu.VMEM((NZ, CHUNK, LANES), F32),
         pltpu.VMEM((512, 3 * LANES), BF),
         pltpu.VMEM((512 + 2 * RF, 512), F32),
-        pltpu.VMEM((2, RF, 512), F32),
-        pltpu.VMEM((2, RF, 512), F32),
-        dma((2,)),
+        pltpu.VMEM((512, 512), F32),
+        pltpu.SemaphoreType.REGULAR, dma((6,)), dma((2,)),
         dma((NZ,)), dma((NZ,)), dma((NZ,)), dma((NZ,)), dma((2, NZ)), dma((2, NZ)),
         dma((NPLANE,)), dma((NPLANE,)), dma((NPLANE,)), dma((NPLANE,)), dma, dma, dma((16,)), dma((16,)),
-        dma((2, 4, 2)), dma((2, 4, 2)), dma((2,)), dma((2,)),
+        dma((2, 4, 4)), dma((2, 4, 4)), dma((2,)), dma((2,)), dma((2,)),
     ]
-    return pl.pallas_call(
+    coadd, rows = pl.pallas_call(
         kernel,
-        out_shape=(jax.ShapeDtypeStruct((512, 512), F32), jax.ShapeDtypeStruct((512, 512), F32)),
-        in_specs=[hbm, hbm, vmem, vmem, vmem, smem, smem, smem],
-        out_specs=(vmem, vmem),
+        out_shape=(jax.ShapeDtypeStruct((512, 512), F32), jax.ShapeDtypeStruct((512 + 2 * RF, 512), F32)),
+        in_specs=[hbm] * 8,
+        out_specs=(hbm, hbm),
         scratch_shapes=scratch,
         compiler_params=pltpu.CompilerParams(
-            collective_id=0, has_side_effects=True, vmem_limit_bytes=40 * 1024 * 1024),
-    )(cells, variance, coefficients, band_offsets, shifts, destination, position, psf_taps)
+            collective_id=0, has_side_effects=True, vmem_limit_bytes=60 * 1024 * 1024),
+    )(cells, variance, coefficients, band_offsets.T, shifts.T, destination, position, psf_taps)
+    return pl.pallas_call(
+        filter_rows,
+        out_shape=(jax.ShapeDtypeStruct((512, 512), F32), jax.ShapeDtypeStruct((512, 512), F32)),
+        in_specs=[hbm, hbm, hbm],
+        out_specs=(hbm, hbm),
+        scratch_shapes=[
+            pltpu.SMEM((2 * RF + 1,), F32), pltpu.VMEM((512 + 2 * RF, 512), F32), pltpu.VMEM((512, 512), F32),
+            pltpu.VMEM((512, 512), F32), dma((6,)), dma((5,))],
+        compiler_params=pltpu.CompilerParams(vmem_limit_bytes=60 * 1024 * 1024),
+    )(psf_taps, coadd, rows)
 
 
 def solution(mesh):

time: 85.2 us -> 73.4 us (0.86)
  the two profiles are of different devices: /device:TPU:2 before, /device:TPU:104 now
where the time goes in v1:
time: 73.4 us; the launch traced here: 73.2 us
  Pallas kernels  72.6 us (99%)
    pallas_call x1, Pallas kernels, body(): pl.pallas_call(kernel, out_shape=(jax.ShapeDtypeStruct((512, 512), F32),...  69.7 us
    pallas_call x1, Pallas kernels, body(): pl.pallas_call(filter_rows, out_shape=(jax.ShapeDtypeStruct((512, 512), F...  2.9 us

profile of v1, /device:TPU:104, one launch (start us, length us, event | category | flops | bytes accessed | tf_op | source)
XLA Modules:
  0.0 73.2 jit_solution(14566009182503805176)
XLA Ops:
  0.6 69.7 %shard_map.95 = (f32[512,512]{1,0:T(8,128)}, f32[528,512]{1,0:T(8,128)}) custom-call(f32[2304,128]{1,0:T(8,128)} %bitcast.7, f32[8,128,128]{2,1,0:T(8,128)} %var_ref.1, f32[8,9]{1,0:T(8,128)} %coef_hbm.1, s32[2,8]{1,0:T(2,128)} %bitcast.8, f32[2,8]{1,0:T(2,128)} %bitcast.9, s32[8]{0:T(128)} %dest_hbm.1, s32[8]{0:T(128)} %pos_hbm.1, f32[17]{0:T(128)} %taps_hbm.3), custom_call_target="tpu_custom_call" | custom-call | tf_op jit(solution)/shard_map/pallas_call | solution.py:632
  70.3 2.9 %shard_map.96 = (f32[512,512]{1,0:T(8,128)}, f32[512,512]{1,0:T(8,128)}) custom-call(f32[17]{0:T(128)} %taps_hbm.3, f32[512,512]{1,0:T(8,128)} %get-tuple-element.4.cells_hbm, f32[528,512]{1,0:T(8,128)} %get-tuple-element.5.rows_hbm), custom_call_target="tpu_custom_call" | custom-call | tf_op jit(solution)/shard_map/pallas_call | solution.py:641

commit v2 on v1

--- a/solution.py
+++ b/solution.py
@@ -22,7 +22,9 @@
 WIDTHS = (1.0, 2.0, 4.0)
 TAPS = (-2, -1, 0, 1, 2, 3)
 CHUNK = 264
-PARTS = ((0, 64), (64, 64), (128, 64), (192, 72))
+PARTS = ((0, 64), (64, 64), (128, 64), (192, 64), (256, 8))
+HALF = 64
+BOTH_WAYS = (1, 7, 2, 6, 3, 5, 4)
 BF = jnp.bfloat16
 F32 = jnp.float32
 
@@ -134,8 +136,7 @@
             zb[at : at + 96, LANES : 2 * LANES] = zl[:, j * LANES : (j + 1) * LANES]
     both = mm(lh[...], zb[...])
     out = both[:, 0:LANES] + both[:, LANES:] + mm(ll[...], zb[:, 0:LANES])
-    flux_ref[k, 0] = out[0:64]
-    flux_ref[k, 1] = out[64:128]
+    flux_ref[pl.ds(k, 128, 8), :] = out
 
 
 def filter_blocks(taps_ref, transposed):
@@ -156,17 +157,16 @@
     coadd_hbm, rows_hbm,
     coef_ref, off_ref, shift_ref, dest_ref, pos_ref, taps_ref,
     stamps_ref, base_ref, mh, ml, lh, ll, zb, flux_ref,
-    ids_z, zw, zf, ids_in, send_w, send_f, landed, onehot, data,
-    sums, mate, half_ref, msg, ret, chunks, xbuf, ybuf, coadd_ref,
+    ids_z, zw, zf, ids_in, weights, pack_w, pack_f, landed_w, landed_f, onehot, data,
+    sums, msg, side_out, side_in, chunks, xbuf, ybuf, coadd_ref,
     seen, small_sem, local_sem, zw_send, zw_recv, zi_send, zi_recv, zf_send, zf_recv,
-    id_send, id_recv, in_send, in_recv, mate_send, mate_recv, ret_send, ret_recv,
+    id_send, id_recv, in_send, in_recv, side_send, side_recv, ret_send, ret_recv,
     ring_send, ring_recv, halo_send, halo_recv, out_sem,
 ):
     z = lax.axis_index("visit")
     y = lax.axis_index("prow")
     p = lax.axis_index("pcol")
     j = y * NP + p
-    r = j // 2
     core = lax.rem(p, 2)
     small = [
         pltpu.make_async_copy(far, near, small_sem.at[i])
@@ -217,7 +217,7 @@
     def z_flux(e, d):
         to = lax.rem(z + d, NZ)
         return pltpu.make_async_remote_copy(
-            src_ref=flux_ref.at[:, e, pl.ds(pl.multiple_of(to * 8, 8), 8), :], dst_ref=zf.at[e, z],
+            src_ref=flux_ref.at[pl.ds(pl.multiple_of(e * 512 + to * 64, 64), 64), :], dst_ref=zf.at[e, z],
             send_sem=zf_send.at[e, d], recv_sem=zf_recv.at[e, z], device_id=(to, y, p), device_id_type=MESH)
 
     def wait_z(recv, dst):
@@ -229,8 +229,7 @@
     def _(d):
         z_ids(d).start()
 
-    @pl.loop(1, NZ)
-    def _(d):
+    for d in BOTH_WAYS:
         z_var(d).start()
 
     @later.append
@@ -260,10 +259,10 @@
     def _(k):
         warp_block(k, stamps_ref, base_ref, mh, ml, lh, ll, zb, flux_ref)
 
+    pl.semaphore_wait(seen, NY - 1)
+
     for e in range(2):
-
-        @pl.loop(1, NZ)
-        def _(d):
+        for d in BOTH_WAYS:
             z_flux(e, d).start()
 
     @later.append
@@ -274,18 +273,18 @@
                 z_flux(e, d).wait_send()
 
     wait_z(zi_recv, ids_z)
-    lane64 = lax.rem(lax.broadcasted_iota(jnp.int32, (64, LANES), 1), 64)
-    row64 = lax.broadcasted_iota(jnp.int32, (64, LANES), 0)
-    picked = jnp.where(lane64 == row64, ids_z[...].reshape(64, LANES), 0.0)
-    ids_in[j] = jnp.broadcast_to(jnp.sum(picked, axis=0, keepdims=True), (8, LANES))
+    lane32 = lax.rem(lax.broadcasted_iota(jnp.int32, (32, LANES), 1), 32)
+    row32 = lax.broadcasted_iota(jnp.int32, (32, LANES), 0)
+    column_ids = ids_z[...].reshape(64, LANES)
+    low_ids = jnp.sum(jnp.where(lane32 == row32, column_ids[0:32], 0.0), axis=0, keepdims=True)
+    high_ids = jnp.sum(jnp.where(lane32 == row32, column_ids[32:64], 0.0), axis=0, keepdims=True)
+    ids_in[j] = jnp.where(lax.broadcasted_iota(jnp.int32, (8, LANES), 0) == 0, low_ids, high_ids)
 
     def in_ids(d):
         other = lax.rem(j + d, NPLANE)
         return pltpu.make_async_remote_copy(
             src_ref=ids_in.at[j], dst_ref=ids_in.at[j], send_sem=id_send.at[d], recv_sem=id_recv.at[j],
             device_id=(z, other // NP, lax.rem(other, NP)), device_id_type=MESH)
-
-    pl.semaphore_wait(seen, NY - 1)
 
     @pl.loop(1, NPLANE)
     def _(d):
@@ -297,149 +296,191 @@
         def _(d):
             in_ids(d).wait_send()
 
-    def in_copy(buf, kind, row):
-        other = 2 * row + kind
-        return pltpu.make_async_remote_copy(
-            src_ref=buf.at[row], dst_ref=landed.at[j], send_sem=in_send.at[other], recv_sem=in_recv.at[j],
-            device_id=(z, other // NP, lax.rem(other, NP)), device_id_type=MESH)
-
-    def own_copy(buf):
-        return pltpu.make_async_copy(buf.at[r], landed.at[j], in_recv.at[j])
+    def in_copy(kind, e, chip):
+        buf, land = ((pack_f, landed_f), (pack_w, landed_w))[kind]
+        other = 2 * chip + e
+        return pltpu.make_async_remote_copy(
+            src_ref=buf.at[e, chip], dst_ref=land.at[j], send_sem=in_send.at[kind, other],
+            recv_sem=in_recv.at[kind, j], device_id=(z, other // NP, lax.rem(other, NP)), device_id_type=MESH)
 
     @later.append
     def _():
         @pl.loop(0, 16)
-        def _(row):
-            for kind, buf in ((0, send_f), (1, send_w)):
-
-                @pl.when(2 * row + kind != j)
+        def _(chip):
+            for e in range(2):
+
+                @pl.when(2 * chip + e != j)
                 def _():
-                    in_copy(buf, kind, row).wait_send()
-
-    def send_rows(buf, kind, first, step):
-        @pl.loop(0, 16 // step)
+                    in_copy(0, e, chip).wait_send()
+                    in_copy(1, e, chip).wait_send()
+
+    def send_rows(kind, e):
+        buf, land = ((pack_f, landed_f), (pack_w, landed_w))[kind]
+
+        @pl.loop(0, 16)
         def _(d):
-            row = lax.rem(r // step + d, 16 // step) * step + first
-            here = 2 * row + kind == j
+            chip = lax.rem(j // 2 + d, 16)
+            here = 2 * chip + e == j
 
             @pl.when(here)
             def _():
-                own_copy(buf).start()
+                pltpu.make_async_copy(buf.at[e, chip], land.at[j], in_recv.at[kind, j]).start()
 
             @pl.when(jnp.logical_not(here))
             def _():
-                in_copy(buf, kind, row).start()
+                in_copy(kind, e, chip).start()
+
+    def wait_rows(kind):
+        land = (landed_f, landed_w)[kind]
+
+        @pl.loop(0, NPLANE)
+        def _(d):
+            other = lax.rem(j + d, NPLANE)
+            pltpu.make_async_copy(land.at[other], land.at[other], in_recv.at[kind, other]).wait()
+
+    first64 = lax.broadcasted_iota(jnp.int32, (8, LANES), 1) < HALF
+
+    def swap(x):
+        return pltpu.roll(x, HALF, 1)
+
+    def pack(buf, e, q, at, low, high):
+        buf[e, 2 * q, at, :] = jnp.where(first64, low, swap(high))
+        buf[e, 2 * q + 1, at, :] = jnp.where(first64, swap(low), high)
 
     wait_z(zw_recv, zw)
     own_var.wait()
-    for source in range(NZ):
-        weight = 1.0 / jnp.swapaxes(zw[source], 0, 1)
-        send_w[:, source * NB : (source + 1) * NB, :] = weight
-    send_rows(send_w, 1, 0, 1)
+    for s in range(4):
+        low = 1.0 / jnp.swapaxes(zw[s], 0, 1)
+        high = 1.0 / jnp.swapaxes(zw[s + 4], 0, 1)
+        for row in range(16):
+            weights[row, s] = low[row]
+            weights[row, s + 4] = high[row]
+            pack(pack_w, row % 2, row // 2, slice(8 * s, 8 * s + 8), low[row], high[row])
+    send_rows(1, 0)
+    send_rows(1, 1)
 
     @pl.loop(1, NPLANE)
     def _(d):
         other = lax.rem(j + d, NPLANE)
         pltpu.make_async_copy(ids_in.at[other], ids_in.at[other], id_recv.at[other]).wait()
 
-    @pl.loop(0, 16)
-    def _(pair):
-        lane = lax.broadcasted_iota(jnp.int32, (8, LANES), 1)
-        mixed = jnp.where(lane < 64, ids_in[2 * pair], ids_in[2 * pair + 1])
+    @pl.loop(0, 8)
+    def _(group):
+        quarter = lax.broadcasted_iota(jnp.int32, (8, LANES), 1) // 32
+        mixed = ids_in[4 * group]
+        for i in range(1, 4):
+            mixed = jnp.where(quarter == i, ids_in[4 * group + i], mixed)
         tile = lax.broadcasted_iota(jnp.int32, (TILES, LANES), 0).astype(F32)
-        onehot[:, pl.ds(pl.multiple_of(pair * LANES, LANES), LANES)] = jnp.where(
-            tile == mixed[0:1], 1.0, 0.0).astype(BF)
+        at = pl.ds(pl.multiple_of(group * LANES, LANES), LANES)
+        for h in range(2):
+            onehot[h, :, at] = jnp.where(tile == mixed[h : h + 1], 1.0, 0.0).astype(BF)
+
+    def tile_sums(land):
+        hi, lo = split(land[...].reshape(NPLANE * 32, LANES))
+        data[:, 0:LANES] = hi
+        data[:, LANES:] = lo
+        low = mm(onehot[0], data[...])
+        high = mm(onehot[1], data[...])
+        return low[:, 0:LANES] + low[:, LANES:] + pltpu.roll(high[:, 0:LANES] + high[:, LANES:], HALF, 1)
 
     col_blocks = jnp.concatenate(filter_blocks(taps_ref, False), axis=0)
     col_hi, col_lo = split(col_blocks)
     col_both = jnp.concatenate([col_hi, col_lo], axis=1)
 
-    for e in range(2):
+    def relay(e):
         wait_z(zf_recv.at[e], zf.at[e])
-        zf[e, z] = flux_ref[:, e, pl.ds(pl.multiple_of(z * 8, 8), 8), :]
-        for source in range(NZ):
-            cells = jnp.swapaxes(zf[e, source], 0, 1)
+        zf[e, z] = flux_ref[pl.ds(pl.multiple_of(e * 512 + z * 64, 64), 64), :]
+        for s in range(4):
             for q in range(8):
-                at = slice(source * NB, (source + 1) * NB)
-                send_f[2 * q + e, at, :] = cells[q] * send_w[2 * q + e, at, :]
-        send_rows(send_f, 0, e, 2)
-
-    @pl.loop(0, NPLANE)
+                row = 2 * q + e
+                low = zf[e, s, 8 * q : 8 * q + 8, :] * weights[row, s]
+                high = zf[e, s + 4, 8 * q : 8 * q + 8, :] * weights[row, s + 4]
+                pack(pack_f, e, q, slice(8 * s, 8 * s + 8), low, high)
+        send_rows(0, e)
+
+    wait_rows(1)
+    sums[...] = 1.0 / (1.0 + tile_sums(landed_w))
+    relay(0)
+    relay(1)
+    wait_rows(0)
+    cells = (tile_sums(landed_f) * sums[...]).reshape(NPLANE, 2, 8, LANES)
+    for o in range(NPLANE):
+        msg[o] = jnp.where(first64, cells[o, 0], swap(cells[o, 1]))
+
+    def ret_copy(o):
+        return pltpu.make_async_remote_copy(
+            src_ref=msg.at[o], dst_ref=chunks.at[z, pl.ds(pl.multiple_of(8 * j, 8), 8), :],
+            send_sem=ret_send.at[o], recv_sem=ret_recv.at[j],
+            device_id=(z, o // NP, lax.rem(o, NP)), device_id_type=MESH)
+
+    pltpu.make_async_copy(
+        msg.at[j], chunks.at[z, pl.ds(pl.multiple_of(8 * j, 8), 8), :], ret_recv.at[j]).start()
+
+    @pl.loop(1, NPLANE)
     def _(d):
-        other = lax.rem(j + d, NPLANE)
-        pltpu.make_async_copy(landed.at[other], landed.at[other], in_recv.at[other]).wait()
-
-    hi, lo = split(landed[...].reshape(NPLANE * 64, LANES))
-    data[:, 0:LANES] = hi
-    data[:, LANES:] = lo
-    total = mm(onehot[...], data[...])
-    sums[...] = total[:, 0:LANES] + total[:, LANES:]
-
-    trade = pltpu.make_async_remote_copy(
-        src_ref=sums.at[pl.ds(pl.multiple_of((1 - core) * 256, 256), 256), :], dst_ref=mate,
-        send_sem=mate_send, recv_sem=mate_recv, device_id=(z, y, p + 1 - 2 * core), device_id_type=MESH)
-    trade.start()
-    later.append(trade.wait_send)
-    half_ref[0:16, :] = jnp.zeros((16, LANES), F32)
-    half_ref[272:288, :] = jnp.zeros((16, LANES), F32)
-    own = sums[pl.ds(pl.multiple_of(core * 256, 256), 256), :]
-    trade.wait_recv()
-    theirs = mate[...]
-    half_ref[16:272, :] = jnp.where(core == 0, own, theirs) / (1.0 + jnp.where(core == 0, theirs, own))
-
-    patch = lax.rem(lax.broadcasted_iota(jnp.int32, (64, LANES), 0) // 4, NP)
-    lane = lax.broadcasted_iota(jnp.int32, (64, LANES), 1)
-    right = half_ref[pl.ds(32, 64, 4), :]
-    left = half_ref[pl.ds(3, 64, 4), :]
-    beside = jnp.where((lane < RF) & (patch < NP - 1), right, 0.0)
-    beside = jnp.where((lane >= LANES - RF) & (patch > 0), left, beside)
-    for m in range(16):
-        msg[m, 0:16, :] = half_ref[16 + 16 * m : 32 + 16 * m, :]
-        msg[m, 16:20, :] = beside[4 * m : 4 * m + 4]
-        msg[m, 20:24, :] = jnp.zeros((4, LANES), F32)
-
-    def ret_copy(m):
-        return pltpu.make_async_remote_copy(
-            src_ref=msg.at[m], dst_ref=ret.at[r], send_sem=ret_send.at[m], recv_sem=ret_recv.at[r],
-            device_id=(z, 2 * core + m // 8, lax.rem(m, 8)), device_id_type=MESH)
-
-    def each_owner(far, near):
-        @pl.loop(0, 16)
+        ret_copy(lax.rem(j + d, NPLANE)).start()
+
+    @later.append
+    def _():
+        @pl.loop(1, NPLANE)
         def _(d):
-            m = lax.rem(r + d, 16)
-            here = jnp.logical_and(2 * core + m // 8 == y, lax.rem(m, 8) == p)
-
-            @pl.when(here)
+            ret_copy(lax.rem(j + d, NPLANE)).wait_send()
+
+    def wait_ret(first, count):
+        @pl.loop(first, first + count)
+        def _(s):
+            ref = chunks.at[z, pl.ds(pl.multiple_of(8 * s, 8), 8), :]
+            pltpu.make_async_copy(ref, ref, ret_recv.at[s]).wait()
+
+    def assembled(which):
+        cell_rows = []
+        for row in range(16):
+            e, q = row % 2, row // 2
+            one = chunks[which, 8 * (4 * q + e) : 8 * (4 * q + e) + 8, :]
+            two = chunks[which, 8 * (4 * q + 2 + e) : 8 * (4 * q + 2 + e) + 8, :]
+            cell_rows.append(jnp.concatenate(
+                [jnp.where(first64, one, swap(two)), jnp.where(first64, swap(one), two)], axis=0)[None])
+        return jnp.swapaxes(jnp.concatenate(cell_rows, axis=0), 0, 1)
+
+    def side_copy(side):
+        return pltpu.make_async_remote_copy(
+            src_ref=side_out.at[side], dst_ref=side_in.at[1 - side], send_sem=side_send.at[side],
+            recv_sem=side_recv.at[1 - side], device_id=(z, y, p - 1 + 2 * side), device_id_type=MESH)
+
+    def beside(side):
+        return p > 0 if side == 0 else p < NP - 1
+
+    def send_sides(got):
+        lane8 = lax.broadcasted_iota(jnp.int32, (8, LANES), 1)
+        to_left = jnp.zeros((8, LANES), F32)
+        to_right = jnp.zeros((8, LANES), F32)
+        for g in range(8):
+            rows = slice(8 * (g % 2), 8 * (g % 2) + 8)
+            at = (8 + 16 * g) % LANES
+            to_left = to_left + pltpu.roll(jnp.where(lane8 < RF, got[4 * (g // 2), rows, :], 0.0), at, 1)
+            to_right = to_right + pltpu.roll(
+                jnp.where(lane8 >= LANES - RF, got[4 * (g // 2) + 3, rows, :], 0.0), at, 1)
+        side_out[0] = to_left
+        side_out[1] = to_right
+        for side in range(2):
+
+            @pl.when(beside(side))
             def _():
-                near(m)
-
-            @pl.when(jnp.logical_not(here))
+                side_copy(side).start()
+
+    @later.append
+    def _():
+        for side in range(2):
+
+            @pl.when(beside(side))
             def _():
-                far(m)
-
-    each_owner(
-        lambda m: ret_copy(m).start(),
-        lambda m: pltpu.make_async_copy(msg.at[m], ret.at[r], ret_recv.at[r]).start())
-
-    later.append(lambda: each_owner(lambda m: ret_copy(m).wait_send(), lambda m: None))
-
-    @pl.loop(0, 16)
-    def _(s):
-        pltpu.make_async_copy(ret.at[s], ret.at[s], ret_recv.at[s]).wait()
-
-    got = jnp.swapaxes(ret[...], 0, 1)
-    mine = chunks.at[z]
-    for t in range(16):
-        mine[16 * t : 16 * t + 16, :] = got[t]
-    packed = jnp.zeros((8, LANES), F32)
-    for g in range(8):
-        packed = packed + pltpu.roll(got[16 + g // 2, 8 * (g % 2) : 8 * (g % 2) + 8, :], (8 + 16 * g) % LANES, 1)
-    mine[256:264, :] = packed
+                side_copy(side).wait_send()
 
 
     def ring(way, step, part):
-        which = lax.rem(z - step + NZ, NZ) if way == 0 else lax.rem(z + step, NZ)
-        to = lax.rem(z + 1, NZ) if way == 0 else lax.rem(z + NZ - 1, NZ)
+        back, hop = (step, 1) if step < 3 else (2, 2)
+        which = lax.rem(z - back + NZ, NZ) if way == 0 else lax.rem(z + back, NZ)
+        to = lax.rem(z + hop, NZ) if way == 0 else lax.rem(z + NZ - hop, NZ)
         at, size = PARTS[part]
         ref = chunks.at[which, pl.ds(at, size), :]
         return pltpu.make_async_remote_copy(
@@ -452,23 +493,29 @@
         ref = chunks.at[which, pl.ds(at, size), :]
         pltpu.make_async_copy(ref, ref, ring_recv.at[way, step, part]).wait()
 
-    def halo(side):
+    def halo(side, far):
         mine, theirs = (RF, 512 + RF) if side == 0 else (512, 0)
         return pltpu.make_async_remote_copy(
             src_ref=ybuf.at[pl.ds(mine, RF), :], dst_ref=ybuf.at[pl.ds(theirs, RF), :],
-            send_sem=halo_send.at[side], recv_sem=halo_recv.at[1 - side],
-            device_id=(z, y - 1 + 2 * side, p), device_id_type=MESH)
+            send_sem=halo_send.at[side, far], recv_sem=halo_recv.at[1 - side],
+            device_id=(lax.rem(z + 4 * far, NZ), y - 1 + 2 * side, p), device_id_type=MESH)
+
+    def halo_goes(side, far):
+        there = y > 0 if side == 0 else y < NY - 1
+        first = 0 if side == 0 else NZ - 1
+        return jnp.logical_and(there, z == first if far else z != (first + 4) % NZ)
 
     def filter_chunk(which):
-        chunk = chunks[which]
+        cells = assembled(which)
+        packed = chunks[which, 256:264, :]
         lane8 = lax.broadcasted_iota(jnp.int32, (8, LANES), 1)
         for pr in range(4):
             beside = []
             for h in range(2):
-                rolled = pltpu.roll(chunk[256:264], (LANES - 8 - 16 * (2 * pr + h)) % LANES, 1)
+                rolled = pltpu.roll(packed, (LANES - 8 - 16 * (2 * pr + h)) % LANES, 1)
                 beside.append(jnp.where((lane8 < RF) | (lane8 >= LANES - RF), rolled, 0.0))
             beside = jnp.concatenate(beside, axis=0)
-            tiles = [chunk[(4 * pr + pc) * 16 : (4 * pr + pc) * 16 + 16] for pc in range(4)]
+            tiles = [cells[4 * pr + pc] for pc in range(4)]
             at = pl.ds(pl.multiple_of(pr * 128 + which * 16, 16), 16)
             for pc in range(4):
                 coadd_ref[at, pc * LANES : (pc + 1) * LANES] = tiles[pc]
@@ -487,23 +534,24 @@
         for pr in range(4):
             at = pl.ds(pl.multiple_of(pr * 128 + which * 16, 16), 16)
             pltpu.make_async_copy(coadd_ref.at[at, :], coadd_hbm.at[at, :], out_sem.at[0]).start()
-
-        @pl.when(jnp.logical_and(which == 0, y > 0))
-        def _():
-            halo(0).start()
-
-        @pl.when(jnp.logical_and(which == NZ - 1, y < NY - 1))
-        def _():
-            halo(1).start()
+            at = pl.ds(pl.multiple_of(RF + pr * 128 + which * 16, 8), 16)
+            pltpu.make_async_copy(ybuf.at[at, :], rows_hbm.at[at, :], out_sem.at[1]).start()
+
+        for side, number in ((0, 0), (1, NZ - 1)):
+            for far in range(2):
+
+                @pl.when(jnp.logical_and(which == number, halo_goes(side, far)))
+                def _():
+                    halo(side, far).start()
 
     def passes(way, step, part):
-        return step < 3 or part // 2 == way
+        return step < 3 or (part < 2) == (way == 0)
 
     @later.append
     def _():
         for way in range(2):
             for step in range(4):
-                for part in range(4):
+                for part in range(5):
                     if passes(way, step, part):
                         ring(way, step, part).wait_send()
 
@@ -511,49 +559,72 @@
         for way in range(2):
             if passes(way, step - 1, part):
                 came(way, step - 1, part)
-                if step < 4 and passes(way, step, part):
+                if step == 2 and passes(way, 3, part):
+                    ring(way, 3, part).start()
+                if step < 3:
                     ring(way, step, part).start()
 
     for part in range(4):
+        wait_ret(8 * part, 8)
         ring(0, 0, part).start()
         ring(1, 0, part).start()
+    send_sides(assembled(z))
+    chunks[z, 256:264, :] = jnp.zeros((8, LANES), F32)
+    for side in range(2):
+
+        @pl.when(beside(side))
+        def _():
+            side_copy(1 - side).wait_recv()
+            chunks[z, 256:264, :] += side_in[side]
+
+    ring(0, 0, 4).start()
+    ring(1, 0, 4).start()
+    for part in range(4):
+        advance(1, part)
     filter_chunk(z)
-    for step in range(1, 5):
-        for part in range(4):
-            advance(step, part)
-            if step > 1 and part == 1:
-                filter_chunk(lax.rem(z - step + 1 + NZ, NZ))
-        if step > 1:
-            filter_chunk(lax.rem(z + step - 1, NZ))
+    advance(1, 4)
+    for part in range(4):
+        advance(2, part)
+    filter_chunk(lax.rem(z - 1 + NZ, NZ))
+    advance(2, 4)
+    filter_chunk(lax.rem(z + 1, NZ))
+    filter_chunk(lax.rem(z - 2 + NZ, NZ))
+    filter_chunk(lax.rem(z + 2, NZ))
+    for part in range(5):
+        advance(3, part)
+    filter_chunk(lax.rem(z - 3 + NZ, NZ))
+    filter_chunk(lax.rem(z + 3, NZ))
+    for part in range(5):
+        advance(4, part)
     filter_chunk(lax.rem(z + 4, NZ))
 
     for side in range(2):
         there = y > 0 if side == 0 else y < NY - 1
-        at = 0 if side == 0 else 512 + RF
+        at = pl.ds(0 if side == 0 else 512 + RF, RF)
 
         @pl.when(there)
         def _():
-            halo(1 - side).wait_recv()
+            halo(1 - side, 0).wait_recv()
 
         @pl.when(jnp.logical_not(there))
         def _():
-            ybuf[at : at + RF, :] = jnp.zeros((RF, 512), F32)
+            ybuf[at, :] = jnp.zeros((RF, 512), F32)
+
+        pltpu.make_async_copy(ybuf.at[at, :], rows_hbm.at[at, :], out_sem.at[1]).start()
 
     @later.append
     def _():
         for side in range(2):
-            there = y > 0 if side == 0 else y < NY - 1
-
-            @pl.when(there)
-            def _():
-                halo(side).wait_send()
-
-    rows_out = pltpu.make_async_copy(ybuf, rows_hbm, out_sem.at[1])
-    rows_out.start()
+            for far in range(2):
+
+                @pl.when(halo_goes(side, far))
+                def _():
+                    halo(side, far).wait_send()
+
     for left in later:
         left()
     pltpu.make_async_copy(coadd_ref, coadd_hbm, out_sem.at[0]).wait()
-    rows_out.wait()
+    pltpu.make_async_copy(ybuf, rows_hbm, out_sem.at[1]).wait()
 
 
 def filter_rows(taps_hbm, cells_hbm, rows_hbm, coadd_hbm, det_hbm, taps_ref, rows_ref, cells_ref, det_ref, in_sem, out_sem):
@@ -605,29 +676,30 @@
         pltpu.VMEM((LANES, 12 * LANES), BF),
         pltpu.VMEM((LANES, 12 * LANES), BF),
         pltpu.VMEM((12 * LANES, 2 * LANES), BF),
-        pltpu.VMEM((NB, 2, 64, LANES), F32),
+        pltpu.VMEM((NB * LANES, LANES), F32),
         pltpu.VMEM((NZ, NB, LANES), F32),
         pltpu.VMEM((NZ, NB, 16, LANES), F32),
-        pltpu.VMEM((2, NZ, NB, 8, LANES), F32),
+        pltpu.VMEM((2, NZ, 64, LANES), F32),
         pltpu.VMEM((NPLANE, 8, LANES), F32),
-        pltpu.VMEM((16, 64, LANES), F32),
-        pltpu.VMEM((16, 64, LANES), F32),
-        pltpu.VMEM((NPLANE, 64, LANES), F32),
-        pltpu.VMEM((TILES, NPLANE * 64), BF),
-        pltpu.VMEM((NPLANE * 64, 2 * LANES), BF),
+        pltpu.VMEM((16, NZ, NB, LANES), F32),
+        pltpu.VMEM((2, 16, 32, LANES), F32),
+        pltpu.VMEM((2, 16, 32, LANES), F32),
+        pltpu.VMEM((NPLANE, 32, LANES), F32),
+        pltpu.VMEM((NPLANE, 32, LANES), F32),
+        pltpu.VMEM((2, TILES, NPLANE * 32), BF),
+        pltpu.VMEM((NPLANE * 32, 2 * LANES), BF),
         pltpu.VMEM((TILES, LANES), F32),
-        pltpu.VMEM((TILES // 2, LANES), F32),
-        pltpu.VMEM((288, LANES), F32),
-        pltpu.VMEM((16, 24, LANES), F32),
-        pltpu.VMEM((16, 24, LANES), F32),
+        pltpu.VMEM((NPLANE, 8, LANES), F32),
+        pltpu.VMEM((2, 8, LANES), F32),
+        pltpu.VMEM((2, 8, LANES), F32),
         pltpu.VMEM((NZ, CHUNK, LANES), F32),
         pltpu.VMEM((512, 3 * LANES), BF),
         pltpu.VMEM((512 + 2 * RF, 512), F32),
         pltpu.VMEM((512, 512), F32),
         pltpu.SemaphoreType.REGULAR, dma((6,)), dma((2,)),
         dma((NZ,)), dma((NZ,)), dma((NZ,)), dma((NZ,)), dma((2, NZ)), dma((2, NZ)),
-        dma((NPLANE,)), dma((NPLANE,)), dma((NPLANE,)), dma((NPLANE,)), dma, dma, dma((16,)), dma((16,)),
-        dma((2, 4, 4)), dma((2, 4, 4)), dma((2,)), dma((2,)), dma((2,)),
+        dma((NPLANE,)), dma((NPLANE,)), dma((2, NPLANE)), dma((2, NPLANE)), dma((2,)), dma((2,)),
+        dma((NPLANE,)), dma((NPLANE,)), dma((2, 4, 5)), dma((2, 4, 5)), dma((2, 2)), dma((2,)), dma((2,)),
     ]
     coadd, rows = pl.pallas_call(
         kernel,

time: 73.4 us -> 71.6 us (0.975)
  the two profiles are of different devices: /device:TPU:104 before, /device:TPU:1 now
where the time goes in v2:
time: 71.6 us; the launch traced here: 71.4 us
  Pallas kernels  70.8 us (99%)
    pallas_call x1, Pallas kernels, body(): pl.pallas_call(kernel, out_shape=(jax.ShapeDtypeStruct((512, 512), F32),...  67.9 us
    pallas_call x1, Pallas kernels, body(): pl.pallas_call(filter_rows, out_shape=(jax.ShapeDtypeStruct((512, 512), F...  2.89 us

profile of v2, /device:TPU:1, one launch (start us, length us, event | category | flops | bytes accessed | tf_op | source)
XLA Modules:
  0.0 71.4 jit_solution(11893249116119179270)
XLA Ops:
  0.6 67.9 %shard_map.95 = (f32[512,512]{1,0:T(8,128)}, f32[528,512]{1,0:T(8,128)}) custom-call(f32[2304,128]{1,0:T(8,128)} %bitcast.7, f32[8,128,128]{2,1,0:T(8,128)} %var_ref.1, f32[8,9]{1,0:T(8,128)} %coef_hbm.1, s32[2,8]{1,0:T(2,128)} %bitcast.8, f32[2,8]{1,0:T(2,128)} %bitcast.9, s32[8]{0:T(128)} %dest_hbm.1, s32[8]{0:T(128)} %pos_hbm.1, f32[17]{0:T(128)} %taps_hbm.3), custom_call_target="tpu_custom_call" | custom-call | tf_op jit(solution)/shard_map/pallas_call | solution.py:704
  68.5 2.9 %shard_map.96 = (f32[512,512]{1,0:T(8,128)}, f32[512,512]{1,0:T(8,128)}) custom-call(f32[17]{0:T(128)} %taps_hbm.3, f32[512,512]{1,0:T(8,128)} %get-tuple-element.4.cells_hbm, f32[528,512]{1,0:T(8,128)} %get-tuple-element.5.rows_hbm), custom_call_target="tpu_custom_call" | custom-call | tf_op jit(solution)/shard_map/pallas_call | solution.py:713

commit v3 on v2

--- a/solution.py
+++ b/solution.py
@@ -205,25 +205,26 @@
 
     def z_ids(d):
         return pltpu.make_async_remote_copy(
-            src_ref=ids_z.at[z], dst_ref=ids_z.at[z], send_sem=zi_send.at[d], recv_sem=zi_recv.at[z],
+            src_ref=ids_z.at[z], dst_ref=ids_z.at[z], send_sem=zi_send, recv_sem=zi_recv,
             device_id=(lax.rem(z + d, NZ), y, p), device_id_type=MESH)
 
     def z_var(d):
         to = lax.rem(z + d, NZ)
         return pltpu.make_async_remote_copy(
             src_ref=var_ref.at[:, pl.ds(pl.multiple_of(to * 16, 16), 16), :], dst_ref=zw.at[z],
-            send_sem=zw_send.at[d], recv_sem=zw_recv.at[z], device_id=(to, y, p), device_id_type=MESH)
+            send_sem=zw_send, recv_sem=zw_recv, device_id=(to, y, p), device_id_type=MESH)
 
     def z_flux(e, d):
         to = lax.rem(z + d, NZ)
         return pltpu.make_async_remote_copy(
             src_ref=flux_ref.at[pl.ds(pl.multiple_of(e * 512 + to * 64, 64), 64), :], dst_ref=zf.at[e, z],
-            send_sem=zf_send.at[e, d], recv_sem=zf_recv.at[e, z], device_id=(to, y, p), device_id_type=MESH)
-
-    def wait_z(recv, dst):
-        for d in range(1, NZ):
-            source = lax.rem(z + d, NZ)
-            pltpu.make_async_copy(dst.at[source], dst.at[source], recv.at[source]).wait()
+            send_sem=zf_send, recv_sem=zf_recv.at[e], device_id=(to, y, p), device_id_type=MESH)
+
+    def wait_bytes(ref, sem):
+        pltpu.make_async_copy(ref, ref, sem).wait()
+
+    def others(buf):
+        return buf.at[pl.ds(0, NZ - 1)]
 
     @pl.loop(1, NZ)
     def _(d):
@@ -234,10 +235,8 @@
 
     @later.append
     def _():
-        @pl.loop(1, NZ)
-        def _(d):
-            z_ids(d).wait_send()
-            z_var(d).wait_send()
+        wait_bytes(others(ids_z), zi_send)
+        wait_bytes(others(zw), zw_send)
 
     own_var = pltpu.make_async_copy(
         var_ref.at[:, pl.ds(pl.multiple_of(z * 16, 16), 16), :], zw.at[z], local_sem.at[1])
@@ -267,12 +266,9 @@
 
     @later.append
     def _():
-        @pl.loop(1, NZ)
-        def _(d):
-            for e in range(2):
-                z_flux(e, d).wait_send()
-
-    wait_z(zi_recv, ids_z)
+        wait_bytes(flux_ref.at[pl.ds(0, 2 * (NZ - 1) * 64), :], zf_send)
+
+    wait_bytes(others(ids_z), zi_recv)
     lane32 = lax.rem(lax.broadcasted_iota(jnp.int32, (32, LANES), 1), 32)
     row32 = lax.broadcasted_iota(jnp.int32, (32, LANES), 0)
     column_ids = ids_z[...].reshape(64, LANES)
@@ -283,7 +279,7 @@
     def in_ids(d):
         other = lax.rem(j + d, NPLANE)
         return pltpu.make_async_remote_copy(
-            src_ref=ids_in.at[j], dst_ref=ids_in.at[j], send_sem=id_send.at[d], recv_sem=id_recv.at[j],
+            src_ref=ids_in.at[j], dst_ref=ids_in.at[j], send_sem=id_send, recv_sem=id_recv,
             device_id=(z, other // NP, lax.rem(other, NP)), device_id_type=MESH)
 
     @pl.loop(1, NPLANE)
@@ -292,27 +288,19 @@
 
     @later.append
     def _():
-        @pl.loop(1, NPLANE)
-        def _(d):
-            in_ids(d).wait_send()
+        wait_bytes(ids_in.at[pl.ds(0, NPLANE - 1)], id_send)
 
     def in_copy(kind, e, chip):
         buf, land = ((pack_f, landed_f), (pack_w, landed_w))[kind]
         other = 2 * chip + e
         return pltpu.make_async_remote_copy(
-            src_ref=buf.at[e, chip], dst_ref=land.at[j], send_sem=in_send.at[kind, other],
-            recv_sem=in_recv.at[kind, j], device_id=(z, other // NP, lax.rem(other, NP)), device_id_type=MESH)
+            src_ref=buf.at[e, chip], dst_ref=land.at[j], send_sem=in_send.at[kind],
+            recv_sem=in_recv.at[kind], device_id=(z, other // NP, lax.rem(other, NP)), device_id_type=MESH)
 
     @later.append
     def _():
-        @pl.loop(0, 16)
-        def _(chip):
-            for e in range(2):
-
-                @pl.when(2 * chip + e != j)
-                def _():
-                    in_copy(0, e, chip).wait_send()
-                    in_copy(1, e, chip).wait_send()
+        wait_bytes(landed_f.at[pl.ds(0, NPLANE - 1)], in_send.at[0])
+        wait_bytes(landed_w.at[pl.ds(0, NPLANE - 1)], in_send.at[1])
 
     def send_rows(kind, e):
         buf, land = ((pack_f, landed_f), (pack_w, landed_w))[kind]
@@ -324,19 +312,14 @@
 
             @pl.when(here)
             def _():
-                pltpu.make_async_copy(buf.at[e, chip], land.at[j], in_recv.at[kind, j]).start()
+                pltpu.make_async_copy(buf.at[e, chip], land.at[j], in_recv.at[kind]).start()
 
             @pl.when(jnp.logical_not(here))
             def _():
                 in_copy(kind, e, chip).start()
 
     def wait_rows(kind):
-        land = (landed_f, landed_w)[kind]
-
-        @pl.loop(0, NPLANE)
-        def _(d):
-            other = lax.rem(j + d, NPLANE)
-            pltpu.make_async_copy(land.at[other], land.at[other], in_recv.at[kind, other]).wait()
+        wait_bytes((landed_f, landed_w)[kind], in_recv.at[kind])
 
     first64 = lax.broadcasted_iota(jnp.int32, (8, LANES), 1) < HALF
 
@@ -347,7 +330,7 @@
         buf[e, 2 * q, at, :] = jnp.where(first64, low, swap(high))
         buf[e, 2 * q + 1, at, :] = jnp.where(first64, swap(low), high)
 
-    wait_z(zw_recv, zw)
+    wait_bytes(others(zw), zw_recv)
     own_var.wait()
     for s in range(4):
         low = 1.0 / jnp.swapaxes(zw[s], 0, 1)
@@ -359,10 +342,7 @@
     send_rows(1, 0)
     send_rows(1, 1)
 
-    @pl.loop(1, NPLANE)
-    def _(d):
-        other = lax.rem(j + d, NPLANE)
-        pltpu.make_async_copy(ids_in.at[other], ids_in.at[other], id_recv.at[other]).wait()
+    wait_bytes(ids_in.at[pl.ds(0, NPLANE - 1)], id_recv)
 
     @pl.loop(0, 8)
     def _(group):
@@ -388,7 +368,7 @@
     col_both = jnp.concatenate([col_hi, col_lo], axis=1)
 
     def relay(e):
-        wait_z(zf_recv.at[e], zf.at[e])
+        wait_bytes(others(zf.at[e]), zf_recv.at[e])
         zf[e, z] = flux_ref[pl.ds(pl.multiple_of(e * 512 + z * 64, 64), 64), :]
         for s in range(4):
             for q in range(8):
@@ -410,11 +390,11 @@
     def ret_copy(o):
         return pltpu.make_async_remote_copy(
             src_ref=msg.at[o], dst_ref=chunks.at[z, pl.ds(pl.multiple_of(8 * j, 8), 8), :],
-            send_sem=ret_send.at[o], recv_sem=ret_recv.at[j],
+            send_sem=ret_send, recv_sem=ret_recv.at[y],
             device_id=(z, o // NP, lax.rem(o, NP)), device_id_type=MESH)
 
     pltpu.make_async_copy(
-        msg.at[j], chunks.at[z, pl.ds(pl.multiple_of(8 * j, 8), 8), :], ret_recv.at[j]).start()
+        msg.at[j], chunks.at[z, pl.ds(pl.multiple_of(8 * j, 8), 8), :], ret_recv.at[y]).start()
 
     @pl.loop(1, NPLANE)
     def _(d):
@@ -422,15 +402,7 @@
 
     @later.append
     def _():
-        @pl.loop(1, NPLANE)
-        def _(d):
-            ret_copy(lax.rem(j + d, NPLANE)).wait_send()
-
-    def wait_ret(first, count):
-        @pl.loop(first, first + count)
-        def _(s):
-            ref = chunks.at[z, pl.ds(pl.multiple_of(8 * s, 8), 8), :]
-            pltpu.make_async_copy(ref, ref, ret_recv.at[s]).wait()
+        wait_bytes(msg.at[pl.ds(0, NPLANE - 1)], ret_send)
 
     def assembled(which):
         cell_rows = []
@@ -477,6 +449,9 @@
                 side_copy(side).wait_send()
 
 
+    def ring_slot(way, step, part):
+        return (3 * way + step) * 5 + part if step < 3 else 30 + part
+
     def ring(way, step, part):
         back, hop = (step, 1) if step < 3 else (2, 2)
         which = lax.rem(z - back + NZ, NZ) if way == 0 else lax.rem(z + back, NZ)
@@ -484,14 +459,14 @@
         at, size = PARTS[part]
         ref = chunks.at[which, pl.ds(at, size), :]
         return pltpu.make_async_remote_copy(
-            src_ref=ref, dst_ref=ref, send_sem=ring_send.at[way, step, part],
-            recv_sem=ring_recv.at[way, step, part], device_id=(to, y, p), device_id_type=MESH)
+            src_ref=ref, dst_ref=ref, send_sem=ring_send,
+            recv_sem=ring_recv.at[ring_slot(way, step, part)], device_id=(to, y, p), device_id_type=MESH)
 
     def came(way, step, part):
         which = lax.rem(z - step - 1 + NZ, NZ) if way == 0 else lax.rem(z + step + 1, NZ)
         at, size = PARTS[part]
         ref = chunks.at[which, pl.ds(at, size), :]
-        pltpu.make_async_copy(ref, ref, ring_recv.at[way, step, part]).wait()
+        pltpu.make_async_copy(ref, ref, ring_recv.at[ring_slot(way, step, part)]).wait()
 
     def halo(side, far):
         mine, theirs = (RF, 512 + RF) if side == 0 else (512, 0)
@@ -549,11 +524,7 @@
 
     @later.append
     def _():
-        for way in range(2):
-            for step in range(4):
-                for part in range(5):
-                    if passes(way, step, part):
-                        ring(way, step, part).wait_send()
+        wait_bytes(others(chunks), ring_send)
 
     def advance(step, part):
         for way in range(2):
@@ -565,7 +536,7 @@
                     ring(way, step, part).start()
 
     for part in range(4):
-        wait_ret(8 * part, 8)
+        wait_bytes(chunks.at[z, pl.ds(64 * part, 64), :], ret_recv.at[part])
         ring(0, 0, part).start()
         ring(1, 0, part).start()
     send_sides(assembled(z))
@@ -697,9 +668,9 @@
         pltpu.VMEM((512 + 2 * RF, 512), F32),
         pltpu.VMEM((512, 512), F32),
         pltpu.SemaphoreType.REGULAR, dma((6,)), dma((2,)),
-        dma((NZ,)), dma((NZ,)), dma((NZ,)), dma((NZ,)), dma((2, NZ)), dma((2, NZ)),
-        dma((NPLANE,)), dma((NPLANE,)), dma((2, NPLANE)), dma((2, NPLANE)), dma((2,)), dma((2,)),
-        dma((NPLANE,)), dma((NPLANE,)), dma((2, 4, 5)), dma((2, 4, 5)), dma((2, 2)), dma((2,)), dma((2,)),
+        dma, dma, dma, dma, dma, dma((2,)),
+        dma, dma, dma((2,)), dma((2,)), dma((2,)), dma((2,)),
+        dma, dma((4,)), dma, dma((35,)), dma((2, 2)), dma((2,)), dma((2,)),
     ]
     coadd, rows = pl.pallas_call(
         kernel,

time: 71.6 us -> 68 us (0.950)
  Pallas kernels: 70.8 us -> 67.2 us
    pallas_call x1, Pallas kernels: 67.9 us -> 64.3 us  [body(): pl.pallas_call(kernel, out_shape=(jax.ShapeDtypeStruct((512, 512), F32),...]
where the time goes in v3:
time: 68 us; the launch traced here: 67.8 us
  Pallas kernels  67.2 us (99%)
    pallas_call x1, Pallas kernels, body(): pl.pallas_call(kernel, out_shape=(jax.ShapeDtypeStruct((512, 512), F32),...  64.3 us
    pallas_call x1, Pallas kernels, body(): pl.pallas_call(filter_rows, out_shape=(jax.ShapeDtypeStruct((512, 512), F...  2.89 us

profile of v3, /device:TPU:1, one launch (start us, length us, event | category | flops | bytes accessed | tf_op | source)
XLA Modules:
  0.0 67.8 jit_solution(5089022436877716988)
XLA Ops:
  0.6 64.3 %shard_map.95 = (f32[512,512]{1,0:T(8,128)}, f32[528,512]{1,0:T(8,128)}) custom-call(f32[2304,128]{1,0:T(8,128)} %bitcast.7, f32[8,128,128]{2,1,0:T(8,128)} %var_ref.1, f32[8,9]{1,0:T(8,128)} %coef_hbm.1, s32[2,8]{1,0:T(2,128)} %bitcast.8, f32[2,8]{1,0:T(2,128)} %bitcast.9, s32[8]{0:T(128)} %dest_hbm.1, s32[8]{0:T(128)} %pos_hbm.1, f32[17]{0:T(128)} %taps_hbm.3), custom_call_target="tpu_custom_call" | custom-call | tf_op jit(solution)/shard_map/pallas_call | solution.py:675
  64.9 2.9 %shard_map.96 = (f32[512,512]{1,0:T(8,128)}, f32[512,512]{1,0:T(8,128)}) custom-call(f32[17]{0:T(128)} %taps_hbm.3, f32[512,512]{1,0:T(8,128)} %get-tuple-element.4.cells_hbm, f32[528,512]{1,0:T(8,128)} %get-tuple-element.5.rows_hbm), custom_call_target="tpu_custom_call" | custom-call | tf_op jit(solution)/shard_map/pallas_call | solution.py:684

commit v4 on v3

--- a/solution.py
+++ b/solution.py
@@ -378,9 +378,9 @@
                 pack(pack_f, e, q, slice(8 * s, 8 * s + 8), low, high)
         send_rows(0, e)
 
+    relay(0)
     wait_rows(1)
     sums[...] = 1.0 / (1.0 + tile_sums(landed_w))
-    relay(0)
     relay(1)
     wait_rows(0)
     cells = (tile_sums(landed_f) * sums[...]).reshape(NPLANE, 2, 8, LANES)

time: 68 us -> 66.5 us (0.978)
  Pallas kernels: 67.2 us -> 65.7 us
    pallas_call x1, Pallas kernels: 64.3 us -> 62.8 us  [body(): pl.pallas_call(kernel, out_shape=(jax.ShapeDtypeStruct((512, 512), F32),...]
where the time goes in v4:
time: 66.5 us; the launch traced here: 66.3 us
  Pallas kernels  65.7 us (99%)
    pallas_call x1, Pallas kernels, body(): pl.pallas_call(kernel, out_shape=(jax.ShapeDtypeStruct((512, 512), F32),...  62.8 us
    pallas_call x1, Pallas kernels, body(): pl.pallas_call(filter_rows, out_shape=(jax.ShapeDtypeStruct((512, 512), F...  2.89 us

profile of v4, /device:TPU:1, one launch (start us, length us, event | category | flops | bytes accessed | tf_op | source)
XLA Modules:
  0.0 66.3 jit_solution(12263599532665029015)
XLA Ops:
  0.6 62.8 %shard_map.95 = (f32[512,512]{1,0:T(8,128)}, f32[528,512]{1,0:T(8,128)}) custom-call(f32[2304,128]{1,0:T(8,128)} %bitcast.7, f32[8,128,128]{2,1,0:T(8,128)} %var_ref.1, f32[8,9]{1,0:T(8,128)} %coef_hbm.1, s32[2,8]{1,0:T(2,128)} %bitcast.8, f32[2,8]{1,0:T(2,128)} %bitcast.9, s32[8]{0:T(128)} %dest_hbm.1, s32[8]{0:T(128)} %pos_hbm.1, f32[17]{0:T(128)} %taps_hbm.3), custom_call_target="tpu_custom_call" | custom-call | tf_op jit(solution)/shard_map/pallas_call | solution.py:675
  63.4 2.9 %shard_map.96 = (f32[512,512]{1,0:T(8,128)}, f32[512,512]{1,0:T(8,128)}) custom-call(f32[17]{0:T(128)} %taps_hbm.3, f32[512,512]{1,0:T(8,128)} %get-tuple-element.4.cells_hbm, f32[528,512]{1,0:T(8,128)} %get-tuple-element.5.rows_hbm), custom_call_target="tpu_custom_call" | custom-call | tf_op jit(solution)/shard_map/pallas_call | solution.py:684

commit v5 on v4

--- a/solution.py
+++ b/solution.py
@@ -379,9 +379,9 @@
         send_rows(0, e)
 
     relay(0)
+    relay(1)
     wait_rows(1)
     sums[...] = 1.0 / (1.0 + tile_sums(landed_w))
-    relay(1)
     wait_rows(0)
     cells = (tile_sums(landed_f) * sums[...]).reshape(NPLANE, 2, 8, LANES)
     for o in range(NPLANE):

time: 66.5 us -> 66.1 us (level)
  no operation moved by 1% of the time
where the time goes in v5:
time: 66.1 us; the launch traced here: 66 us
  Pallas kernels  65.3 us (99%)
    pallas_call x1, Pallas kernels, body(): pl.pallas_call(kernel, out_shape=(jax.ShapeDtypeStruct((512, 512), F32),...  62.4 us
    pallas_call x1, Pallas kernels, body(): pl.pallas_call(filter_rows, out_shape=(jax.ShapeDtypeStruct((512, 512), F...  2.89 us

profile of v5, /device:TPU:1, one launch (start us, length us, event | category | flops | bytes accessed | tf_op | source)
XLA Modules:
  0.0 66.0 jit_solution(3570567008346548934)
XLA Ops:
  0.6 62.4 %shard_map.95 = (f32[512,512]{1,0:T(8,128)}, f32[528,512]{1,0:T(8,128)}) custom-call(f32[2304,128]{1,0:T(8,128)} %bitcast.7, f32[8,128,128]{2,1,0:T(8,128)} %var_ref.1, f32[8,9]{1,0:T(8,128)} %coef_hbm.1, s32[2,8]{1,0:T(2,128)} %bitcast.8, f32[2,8]{1,0:T(2,128)} %bitcast.9, s32[8]{0:T(128)} %dest_hbm.1, s32[8]{0:T(128)} %pos_hbm.1, f32[17]{0:T(128)} %taps_hbm.3), custom_call_target="tpu_custom_call" | custom-call | tf_op jit(solution)/shard_map/pallas_call | solution.py:675
  63.1 2.9 %shard_map.96 = (f32[512,512]{1,0:T(8,128)}, f32[512,512]{1,0:T(8,128)}) custom-call(f32[17]{0:T(128)} %taps_hbm.3, f32[512,512]{1,0:T(8,128)} %get-tuple-element.4.cells_hbm, f32[528,512]{1,0:T(8,128)} %get-tuple-element.5.rows_hbm), custom_call_target="tpu_custom_call" | custom-call | tf_op jit(solution)/shard_map/pallas_call | solution.py:684
